TPU v7x, 256 devices: a whole 4x4x8 slice. The times are simulated.
256 devices in a mesh: dp: 4 (over x), seq: 64 (over y, z, core).
Axes of the slice: x: 4, y: 4, z: 8, core: 2. Of those that a mesh axis runs over, the one named last changes fastest.
Arguments:
- queries: float32 [4, 8192, 768], P('dp', 'seq'), may hold values from -6 to 6
- keys: float32 [4, 8192, 768], P('dp', 'seq'), may hold values from -6 to 6
- values: float32 [4, 8192, 768], P('dp', 'seq'), may hold values from -6 to 6
- out_grad: float32 [4, 8192, 768], P('dp', 'seq'), may hold values from -16 to 16
- out_weight: float32 [768, 768], P(('dp', 'seq')), may hold values from -0.21875 to 0.21875
- valid_tiles: int32 [4], P('dp'), may hold values from 2048 to 8192, as said below
- head_offsets: int32 [12], replicated, may hold values from 0 to 63
Outputs:
- query_grad: float32 [4, 8192, 768], P('dp', 'seq')
- key_grad: float32 [4, 8192, 768], P('dp', 'seq')
- value_grad: float32 [4, 8192, 768], P('dp', 'seq')
- weight_grad: float32 [768, 768], P(('dp', 'seq'))
Inputs may be any that keep to these rules, and one draw needn't show every extreme that they name: The first valid_tiles[s] tiles of slide s are real, the rest padding.
All inputs are finite; a program needn't handle non-finite values.
Results may differ from a plain program's by a relative error of at most 0.0003.
Values sent between devices are 32-bit elements; how exact they have to be, the bound alone decides.
A program may use at most 128 MiB of HBM per device.

v0:
```python
import jax
import jax.numpy as jnp
from jax import lax
from jax.sharding import PartitionSpec as P

HEADS = 12
SEG_DEVICES = 4


PRECISE = lax.Precision.HIGHEST
MASKED = -1e30


def from_partner(block, axis, apart):
    count = lax.axis_size(axis)
    route = []
    for low in range(count):
        high = low | 1 << apart
        if high != low and high < count:
            route += [(low, high), (high, low)]
    return lax.ppermute(block, axis, route)


def elementwise_product(form, left, right):
    return jnp.einsum(form, left, right, precision=PRECISE, preferred_element_type=jnp.float32)


def on_device(queries, keys, values, out_grad, out_weight, valid_tiles, head_offsets):
    slides, block_rows, model_width = queries.shape
    head_size = model_width // HEADS
    spacing = lax.axis_size("seq")
    per_device = block_rows // spacing
    score_scale_factor = head_size ** (-0.5)
    group_bits = SEG_DEVICES.bit_length() - 1
    segment_rows = block_rows * SEG_DEVICES
    seat = lax.axis_index("seq") % SEG_DEVICES
    first_row = lax.axis_index("seq") * block_rows
    positions = first_row + jnp.arange(block_rows, dtype=jnp.int32)
    live_rows = positions[None, :] < valid_tiles[:, None]
    masked_grad = jnp.where(live_rows[:, :, None], out_grad, 0.0).reshape(
        slides * block_rows, model_width
    )
    columns = masked_grad
    attn_grad = jnp.dot(
        columns,
        lax.all_gather(out_weight, ("dp", "seq"), axis=0, tiled=True),
        precision=PRECISE,
        preferred_element_type=jnp.float32,
    )
    query_per_head = queries.reshape(slides, block_rows, HEADS, head_size)
    key_per_head = keys.reshape(slides, block_rows, HEADS, head_size)
    value_per_head = values.reshape(slides, block_rows, HEADS, head_size)
    gradient_per_head = attn_grad.reshape(slides, block_rows, HEADS, head_size)
    key_group, value_group = (key_per_head, value_per_head)
    for bit in range(group_bits):
        other_key, other_value = from_partner((key_group, value_group), "seq", bit)
        upper = seat >> bit & 1 == 1
        key_group = jnp.where(
            upper,
            jnp.concatenate([other_key, key_group], 1),
            jnp.concatenate([key_group, other_key], 1),
        )
        value_group = jnp.where(
            upper,
            jnp.concatenate([other_value, value_group], 1),
            jnp.concatenate([value_group, other_value], 1),
        )
    picker = (jnp.arange(spacing, dtype=jnp.int32)[None, :] == head_offsets[:, None]).astype(
        jnp.float32
    )
    chosen = (jnp.arange(block_rows, dtype=jnp.int32) % spacing)[None, :] == head_offsets[:, None]

    def select_rows(source):
        return elementwise_product(
            "smrhe,hr->shme", source.reshape(slides, per_device, spacing, HEADS, head_size), picker
        )

    def select_scalars(source):
        return elementwise_product(
            "shmr,hr->shm", source.reshape(slides, HEADS, per_device, spacing), picker
        )

    def spread_scalars(source):
        return (source[:, :, :, None] * picker[None, :, None, :]).reshape(slides, HEADS, block_rows)

    def spread_tokens(source):
        return elementwise_product("shme,hr->smrhe", source, picker).reshape(
            slides, block_rows, HEADS, head_size
        )

    segment_start = (lax.axis_index("seq") - seat) * block_rows
    key_positions = segment_start + jnp.arange(segment_rows, dtype=jnp.int32)
    key_live = key_positions[None, :] < valid_tiles[:, None]
    self_keep = (
        jnp.arange(segment_rows, dtype=jnp.int32)[None, :]
        == (seat * block_rows + jnp.arange(block_rows, dtype=jnp.int32))[:, None]
    )
    near_keep = key_live[:, None, None, :] | self_keep[None, None]
    near_scores = jnp.where(
        near_keep,
        elementwise_product("sihe,sjhe->shij", query_per_head, key_group) * score_scale_factor,
        MASKED,
    )
    local_maximum = jnp.max(near_scores, axis=3)
    near_weight = jnp.exp(near_scores - local_maximum[..., None])
    local_total = jnp.sum(near_weight, axis=3)
    near_sum = elementwise_product("shij,sjhe->sihe", near_weight, value_group)
    dilated_query_rows = select_rows(query_per_head)
    dilated_key_rows = select_rows(key_per_head)
    dilated_value_rows = select_rows(value_per_head)
    dilated_gradient = select_rows(gradient_per_head)
    dilated_maximum = select_scalars(local_maximum)
    dilated_total = select_scalars(local_total)
    far_pos = jnp.arange(block_rows, dtype=jnp.int32)[None, :] * spacing + head_offsets[:, None]
    far_live = far_pos[None, :, :] < valid_tiles[:, None, None]
    key_full_rows, value_full_rows = (
        lax.all_gather(dilated_key_rows, "seq", axis=2, tiled=True),
        lax.all_gather(dilated_value_rows, "seq", axis=2, tiled=True),
    )
    distant_score_rows = jnp.where(
        far_live[:, :, None, :],
        elementwise_product("tbkl,tbnl->tbkn", dilated_query_rows, key_full_rows)
        * score_scale_factor,
        MASKED,
    )
    combined_maximum = jnp.maximum(dilated_maximum, jnp.max(distant_score_rows, axis=3))
    distant_weight = jnp.exp(distant_score_rows - combined_maximum[..., None])
    combined_total = dilated_total * jnp.exp(dilated_maximum - combined_maximum) + jnp.sum(
        distant_weight, axis=3
    )
    distant_probability = distant_weight / combined_total[..., None]
    far_out = elementwise_product("shmg,shge->shme", distant_probability, value_full_rows)
    row_top = jnp.where(chosen[None], spread_scalars(combined_maximum), local_maximum)
    row_total = jnp.where(chosen[None], spread_scalars(combined_total), local_total)
    factor = jnp.exp(local_maximum - row_top) / row_total
    near_prob = near_weight * factor[..., None]
    output = near_sum * factor.transpose(0, 2, 1)[..., None] + spread_tokens(far_out)
    attn_flat = output.reshape(slides * block_rows, model_width)
    columns = masked_grad
    weight_sum = lax.psum_scatter(
        lax.dot_general(
            columns,
            attn_flat,
            (((0,), (0,)), ((), ())),
            precision=PRECISE,
            preferred_element_type=jnp.float32,
        ),
        ("dp", "seq"),
        scatter_dimension=0,
        tiled=True,
    )
    weight_grad = weight_sum * (block_rows * spacing) ** (-0.5)
    row_delta_terms = jnp.sum(gradient_per_head * output, axis=3).transpose(0, 2, 1)
    near_ds = near_prob * (
        elementwise_product("sihe,sjhe->shij", gradient_per_head, value_group)
        - row_delta_terms[..., None]
    )
    query_grad = elementwise_product("shij,sjhe->sihe", near_ds, key_group) * score_scale_factor
    key_part = elementwise_product("shij,sihe->sjhe", near_ds, query_per_head) * score_scale_factor
    value_part = elementwise_product("shij,sihe->sjhe", near_prob, gradient_per_head)
    for bit in reversed(range(group_bits)):
        half_rows = key_part.shape[1] // 2
        upper = seat >> bit & 1 == 1
        keep_key = jnp.where(upper, key_part[:, half_rows:], key_part[:, :half_rows])
        send_key = jnp.where(upper, key_part[:, :half_rows], key_part[:, half_rows:])
        keep_value = jnp.where(upper, value_part[:, half_rows:], value_part[:, :half_rows])
        send_value = jnp.where(upper, value_part[:, :half_rows], value_part[:, half_rows:])
        got_key, got_value = from_partner((send_key, send_value), "seq", bit)
        key_part = keep_key + got_key
        value_part = keep_value + got_value
    key_grad = key_part
    value_grad = value_part
    dilated_row_delta = select_scalars(row_delta_terms)
    distant_score_grad = distant_probability * (
        elementwise_product("tbkl,tbnl->tbkn", dilated_gradient, value_full_rows)
        - dilated_row_delta[..., None]
    )
    query_extra = (
        elementwise_product("shmg,shge->shme", distant_score_grad, key_full_rows)
        * score_scale_factor
    )
    key_gradient_terms = (
        elementwise_product("uxln,uxlw->uxnw", distant_score_grad, dilated_query_rows)
        * score_scale_factor
    )
    value_gradient_terms = elementwise_product(
        "uxln,uxlw->uxnw", distant_probability, dilated_gradient
    )
    key_extra, value_extra = (
        lax.psum_scatter(key_gradient_terms, "seq", scatter_dimension=2, tiled=True),
        lax.psum_scatter(value_gradient_terms, "seq", scatter_dimension=2, tiled=True),
    )
    query_grad = (query_grad + spread_tokens(query_extra)).reshape(slides, block_rows, model_width)
    key_grad = (key_grad + spread_tokens(key_extra)).reshape(slides, block_rows, model_width)
    value_grad = (value_grad + spread_tokens(value_extra)).reshape(slides, block_rows, model_width)
    return (query_grad, key_grad, value_grad, weight_grad)


def solution(mesh):
    return jax.shard_map(
        on_device,
        mesh=mesh,
        in_specs=(
            P("dp", "seq", None),
            P("dp", "seq", None),
            P("dp", "seq", None),
            P("dp", "seq", None),
            P(("dp", "seq"), None),
            P("dp"),
            P(),
        ),
        out_specs=(
            P("dp", "seq", None),
            P("dp", "seq", None),
            P("dp", "seq", None),
            P(("dp", "seq"), None),
        ),
        check_vma=False,
    )
```

profile of v0, /device:TPU:1, one launch (start us, length us, event | category | flops | bytes accessed | tf_op | source)
XLA Modules:
  0.0 683.2 jit_solution(17274056988513895126)
XLA Ops:
  9.1 3.3 collective-permute-start.2
  18.6 52.4 %all-gather = f32[12,128,64]{2,0,1:T(8,128)S(1)} all-gather(f32[12,2,64]{2,0,1:T(8,128)S(1)} %bitcast.182), channel_id=2, replica_groups=mesh['dp'=4,'seq'=64] {'seq'}, dimensions={1}, use_global_device_ids=true | all-gather | bytes 399360 | tf_op jit(solution)/shard_map/all_gather | solution.py:117
  75.6 67.3 %all-gather.1 = f32[12,128,64]{2,0,1:T(8,128)} all-gather(f32[12,2,64]{2,0,1:T(8,128)S(1)} %bitcast.181), channel_id=3, replica_groups=mesh['dp'=4,'seq'=64] {'seq'}, dimensions={1}, use_global_device_ids=true | all-gather | bytes 399360 | tf_op jit(solution)/shard_map/all_gather | solution.py:118
  145.9 2.1 fusion.78
  151.9 2.4 maximum_select_fusion.9
  154.2 7.1 %fusion.2 = (f32[12,128]{1,0:T(8,128)}, f32[12,512,128]{2,1,0:T(8,128)S(1)}) fusion(pred[128,512]{0,1:T(8,128)(4,1)} %fusion.39, f32[128,12,64]{0,2,1:T(8,128)S(1)} %bitcast.171, f32[256,12,64]{0,2,1:T(8,128)S(1)} %maximum_select_fusion.7, f32[256,12,64]{0,2,1:T(8,128)} %bitcast.1, pred[]{:T(512)S(6)} %eq.76), kind=kOutput, calls=%fused_computation.5 | convolution fusion | flops 607517184 | bytes 5183489 | tf_op jit(solution)/shard_map/sihe,sjhe->shij/dot_general | solution.py:25
  165.1 2.7 fusion.29
  169.7 2.3 reshape.735
  173.4 4.6 reshape.752
  178.0 5.7 fusion.35
  185.1 2.1 fusion.22
  187.8 2.3 convolution_bitcast_fusion
  190.2 3.0 copy.111
  193.1 6.1 multiply_reduce_fusion
  200.2 2.7 fusion.12
  207.1 5.8 fusion.4
  213.0 7.3 %subtract_multiply_fusion = f32[12,128,512]{1,2,0:T(8,128)S(1)} fusion(f32[128,12,64]{0,2,1:T(8,128)S(1)} %bitcast.170, f32[12,128]{1,0:T(8,128)S(1)} %bitcast.188, f32[12,128]{1,0:T(8,128)S(1)} %copy-done.26, f32[256,12,64]{0,2,1:T(8,128)S(1)} %copy-done.13, f32[256,12,64]{0,2,1:T(8,128)} %bitcast.18, f32[12,128]{1,0:T(8,128)S(1)} %copy-done.17, ...), kind=kOutput, calls=%fused_computation.1 | convolution fusion | flops 609878016 | bytes 8341505 | tf_op jit(solution)/shard_map/sihe,sjhe->shij/dot_general | solution.py:25
  220.3 3.5 multiply_bitcast_fusion
  230.2 4.7 fusion.33
  234.9 174.4 %all-reduce.9.cloned.1.call-done = (f32[1,12,128,64]{3,0,1,2:T(1,128)}, f32[1,12,128,64]{3,0,1,2:T(1,128)}) async-done(((f32[1,12,128,64]{3,0,1,2:T(1,128)}, f32[1,12,128,64]{3,0,1,2:T(1,128)}), (f32[1,12,128,64]{3,0,1,2:T(1,128)}, f32[1,12,128,64]{3,0,1,2:T(1,128)})) %all-reduce.9.cloned.1.call-update) | async-done | bytes 786448
  414.6 5.7 multiply_bitcast_fusion.1
  424.0 2.3 collective-permute-start.7
  429.2 4.2 fusion.11
  440.3 234.6 %all-reduce.7.cloned.1.call-done = f32[768,768]{1,0:T(8,128)} async-done(((f32[768,768]{1,0:T(8,128)}), f32[768,768]{1,0:T(8,128)}) %all-reduce.7.cloned.1.call-update) | async-done | bytes 2359312
  (158 shorter events, 58.5 us)
Async XLA Ops:
  7.2 8.7 %copy-start.27 = (s32[12]{0:T(128)S(1)}, s32[12]{0:T(128)}, u32[]{:S(2)}) copy-start(s32[12]{0:T(128)} %param.13) | copy-start | bytes 148
  7.2 166.2 %all-gather.5.cloned.1.call-start = ((), (), s32[]{:S(2)}) async-start(), calls=%async_computation | async-start | bytes 3158016 | tf_op jit(solution)/shard_map/all_gather | solution.py:46
  7.9 401.4 %all-reduce.9.cloned.1.call-start = ((), (), s32[]{:S(2)}) async-start(), calls=%async_computation.2 | async-start | bytes 3145728
  9.1 139.0 %collective-permute-start.2 = (f32[1,128,12,64]{1,3,2,0:T(8,128)S(1)}, f32[1,128,12,64]{1,3,2,0:T(8,128)}, u32[]{:S(2)}, u32[]{:S(2)}) collective-permute-start(f32[1,128,12,64]{1,3,2,0:T(8,128)S(1)} %bitcast.162), channel_id=1, source_target_pairs={{0,1},{1,0},{2,3},{3,2},{4,5},{5,4},{6,7},{7,6},{8,9},{9,8},{10,11... | collective-permute-start | bytes 1179656 | tf_op jit(solution)/shard_map/ppermute | solution.py:21
  13.6 60.0 %collective-permute-start = (f32[1,128,12,64]{1,3,2,0:T(8,128)S(1)}, f32[1,128,12,64]{1,3,2,0:T(8,128)}, u32[]{:S(2)}, u32[]{:S(2)}) collective-permute-start(f32[1,128,12,64]{1,3,2,0:T(8,128)S(1)} %bitcast.165), channel_id=1, source_target_pairs={{0,1},{1,0},{2,3},{3,2},{4,5},{5,4},{6,7},{7,6},{8,9},{9,8},{10,11... | collective-permute-start | bytes 1179656 | tf_op jit(solution)/shard_map/ppermute | solution.py:21
  18.6 125.6 %copy-start.34 = (u32[256]{0:T(256)S(1)}, u32[256]{0:T(256)}, u32[]{:S(2)}) copy-start(u32[256]{0:T(256)} %constant.61) | copy-start | bytes 3076
  71.0 77.1 %copy-start.5 = (f32[12,128,64]{2,0,1:T(8,128)}, f32[12,128,64]{2,0,1:T(8,128)S(1)}, u32[]{:S(2)}) copy-start(f32[12,128,64]{2,0,1:T(8,128)S(1)} %all-gather) | copy-start | bytes 1179652
  73.6 78.3 %copy-start.21 = (f32[12,1,2,64]{3,1,2,0:T(1,128)}, f32[12,1,2,64]{3,1,2,0:T(1,128)S(1)}, u32[]{:S(2)}) copy-start(f32[12,1,2,64]{3,1,2,0:T(1,128)S(1)} %fusion.20) | copy-start | bytes 18436
  74.8 79.5 %collective-permute-start.1 = (f32[1,256,12,64]{1,3,2,0:T(8,128)S(1)}, f32[1,256,12,64]{1,3,2,0:T(8,128)}, u32[]{:S(2)}, u32[]{:S(2)}) collective-permute-start(f32[1,256,12,64]{1,3,2,0:T(8,128)S(1)} %maximum_select_fusion.6), channel_id=1, source_target_pairs={{0,2},{2,0},{1,3},{3,1},{4,6},{6,4},{5,7},{7,5},{8,10},{10,8},{9,1... | collective-permute-start | bytes 2359304 | tf_op jit(solution)/shard_map/ppermute | solution.py:21
  144.1 17.3 %copy-start.10 = (f32[1,128,768]{1,2,0:T(8,128)}, f32[1,128,768]{1,2,0:T(8,128)S(1)}, u32[]{:S(2)}) copy-start(f32[1,128,768]{1,2,0:T(8,128)S(1)} %copy.88) | copy-start | bytes 1179652
  150.2 42.9 %collective-permute-start.3 = (f32[1,256,12,64]{1,3,2,0:T(8,128)}, f32[1,256,12,64]{1,3,2,0:T(8,128)}, u32[]{:S(2)}, u32[]{:S(2)}) collective-permute-start(f32[1,256,12,64]{1,3,2,0:T(8,128)} %maximum_select_fusion.8), channel_id=1, source_target_pairs={{0,2},{2,0},{1,3},{3,1},{4,6},{6,4},{5,7},{7,5},{8,10},{10,8},{9,1... | collective-permute-start | bytes 2359304 | tf_op jit(solution)/shard_map/ppermute | solution.py:21
  151.9 9.5 %copy-start.8 = (f32[256,12,64]{0,2,1:T(8,128)}, f32[256,12,64]{0,2,1:T(8,128)S(1)}, u32[]{:S(2)}) copy-start(f32[256,12,64]{0,2,1:T(8,128)S(1)} %maximum_select_fusion.7) | copy-start | bytes 2359300
  161.4 31.7 %copy-start = (f32[12,512,128]{2,1,0:T(8,128)}, f32[12,512,128]{2,1,0:T(8,128)S(1)}, u32[]{:S(2)}) copy-start(f32[12,512,128]{2,1,0:T(8,128)S(1)} %get-tuple-element.33) | copy-start | bytes 9437188
  162.3 9.8 %copy-start.16 = (f32[12,128]{1,0:T(8,128)S(1)}, f32[12,128]{1,0:T(8,128)}, u32[]{:S(2)}) copy-start(f32[12,128]{1,0:T(8,128)} %get-tuple-element.32) | copy-start | bytes 18436
  162.3 9.8 %copy-start.28 = (s32[12]{0:T(128)S(1)}, s32[12]{0:T(128)}, u32[]{:S(2)}) copy-start(s32[12]{0:T(128)} %param.13) | copy-start | bytes 148
  162.3 9.8 %copy-start.30 = (s32[128]{0:T(128)S(1)}, s32[128]{0:T(128)}, u32[]{:S(2)}) copy-start(s32[128]{0:T(128)} %and_select_fusion) | copy-start | bytes 1540
  164.3 9.1 %copy-start.15 = (f32[12,2]{1,0:T(8,128)}, f32[12,2]{1,0:T(8,128)S(1)}, u32[]{:S(2)}) copy-start(f32[12,2]{1,0:T(8,128)S(1)} %bitcast_maximum_fusion) | copy-start | bytes 292
  164.7 8.7 %copy-start.18 = (f32[12,2]{1,0:T(8,128)}, f32[12,2]{1,0:T(8,128)S(1)}, u32[]{:S(2)}) copy-start(f32[12,2]{1,0:T(8,128)S(1)} %fusion.59) | copy-start | bytes 292
  225.9 448.9 %all-reduce.7.cloned.1.call-start = ((), (), s32[]{:S(2)}) async-start(), calls=%async_computation.1 | async-start | bytes 4718592
  228.3 193.5 %collective-permute-start.6 = (f32[1,256,12,64]{1,3,2,0:T(8,128)}, f32[1,256,12,64]{1,3,2,0:T(8,128)}, u32[]{:S(2)}, u32[]{:S(2)}) collective-permute-start(f32[1,256,12,64]{1,3,2,0:T(8,128)} %slice_select_fusion), channel_id=1, source_target_pairs={{0,2},{2,0},{1,3},{3,1},{4,6},{6,4},{5,7},{7,5},{8,10},{10,8},{9,1... | collective-permute-start | bytes 2359304 | tf_op jit(solution)/shard_map/ppermute | solution.py:21
  229.9 196.4 %collective-permute-start.4 = (f32[1,256,12,64]{1,3,2,0:T(8,128)}, f32[1,256,12,64]{1,3,2,0:T(8,128)}, u32[]{:S(2)}, u32[]{:S(2)}) collective-permute-start(f32[1,256,12,64]{1,3,2,0:T(8,128)} %slice_select_fusion.1), channel_id=1, source_target_pairs={{0,2},{2,0},{1,3},{3,1},{4,6},{6,4},{5,7},{7,5},{8,10},{10,8},{9,1... | collective-permute-start | bytes 2359304 | tf_op jit(solution)/shard_map/ppermute | solution.py:21
  230.2 184.3 %copy-start.20 = (f32[12,64]{1,0:T(8,128)S(1)}, f32[12,64]{1,0:T(8,128)}, u32[]{:S(2)}) copy-start(f32[12,64]{1,0:T(8,128)} %get-tuple-element.27) | copy-start | bytes 9220
  424.0 12.3 %collective-permute-start.7 = (f32[1,128,12,64]{1,3,2,0:T(8,128)}, f32[1,128,12,64]{1,3,2,0:T(8,128)}, u32[]{:S(2)}, u32[]{:S(2)}) collective-permute-start(f32[1,128,12,64]{1,3,2,0:T(8,128)} %slice_select_fusion.2), channel_id=1, source_target_pairs={{0,1},{1,0},{2,3},{3,2},{4,5},{5,4},{6,7},{7,6},{8,9},{9,8},{10,11... | collective-permute-start | bytes 1179656 | tf_op jit(solution)/shard_map/ppermute | solution.py:21
  428.4 9.9 %collective-permute-start.5 = (f32[1,128,12,64]{1,3,2,0:T(8,128)}, f32[1,128,12,64]{1,3,2,0:T(8,128)}, u32[]{:S(2)}, u32[]{:S(2)}) collective-permute-start(f32[1,128,12,64]{1,3,2,0:T(8,128)} %slice_select_fusion.3), channel_id=1, source_target_pairs={{0,1},{1,0},{2,3},{3,2},{4,5},{5,4},{6,7},{7,6},{8,9},{9,8},{10,11... | collective-permute-start | bytes 1179656 | tf_op jit(solution)/shard_map/ppermute | solution.py:21
  (22 other events, 119.7 us)
Sparse Core Ops, SparseCore 0:
  11.6 110.1 all-gather.4
  226.1 183.2 all-reduce.8
  414.8 260.0 all-reduce.6
where the time goes:
time: 694 us; the launch traced here: 683 us
  waiting for transfers between devices  410 us (59%)
  blocking collectives  120 us (17%)
  matrix products  62.3 us (9%)
  local copies, waits for them, and re-layouts  35.4 us (5%)
  other arithmetic  30.1 us (4%)
  between operations  16.1 us (2%)
  starting transfers between devices  9.9 us (1%)
    unnamed x5, waiting for transfers between devices  410 us
    all_gather x1, blocking collectives, on_device(): lax.all_gather(dilated_value_rows, 'seq', axis=2, tiled=True)  67.3 us
    all_gather x1, blocking collectives, on_device(): lax.all_gather(dilated_key_rows, 'seq', axis=2, tiled=True)  52.4 us
    dot_general x19, matrix products, elementwise_product(): jnp.einsum(form, left, right, precision=PRECISE, preferred_element_type=j...  51.9 us
    unnamed x79, local copies, waits for them, and re-layouts  14.5 us
  transfers between devices with their start and end apart: 11, of which 2 were waited for; matrix products, arithmetic and copies ran while one was open for 14% of the time, Pallas kernels for 0%

commit v1 on v0

v1 whole, which is shorter than its diff:
```python
import jax
import jax.numpy as jnp
from jax import lax
from jax.experimental import pallas as pl
from jax.experimental.pallas import tpu as pltpu

F32 = jnp.float32
BF16 = jnp.bfloat16
MASKED = -1e30
MESH = pl.DeviceIdType.MESH

X, Y, Z = 4, 4, 8
ROWS = 128
SEATS = 4
SEG = ROWS * SEATS
SPACING = 64
SEGMENTS = 16
FAR = 128
WIDTH = 768
HEADS_HERE = 3
KEYS = SEG + FAR
G_CHUNKS = 2
SENDS = 96


def dot(left, right):
    return lax.dot_general(left, right, (((1,), (0,)), ((), ())), preferred_element_type=F32)


def dot_nt(left, right):
    return lax.dot_general(left, right, (((1,), (1,)), ((), ())), preferred_element_type=F32)


def flip(block):
    return pltpu.roll(block, 64, 1)


def low_lanes(block):
    return lax.broadcasted_iota(jnp.int32, block.shape, 1) < 64


def split(block):
    high = block.astype(BF16).astype(F32)
    return high, block - high


def pair(block, upper):
    high, low = split(block)
    if upper:
        return jnp.where(low_lanes(block), flip(high), low)
    return jnp.where(low_lanes(block), high, flip(low))


def twice(block, upper):
    if upper:
        return jnp.where(low_lanes(block), flip(block), block)
    return jnp.where(low_lanes(block), block, flip(block))


def unfold(packed):
    return jnp.concatenate([packed, flip(packed)], axis=0)


def fold_halves(block):
    return block + flip(block)


def kernel(
    q_in, k_in, v_in, g_in, w_in, valid_ref, offset_ref,
    dq_out, dk_out, dv_out, wg_out,
    q_own, k_own, v_own, q_send, k_send, v_send, q_seg, k_seg, v_seg, g_seg,
    w_seg, w_ring, w_all, w_hi, w_lo, far,
    q4, k4, v4, kt, vt, do4, do_t, attn_t, prob, prob_hi, prob_lo, ds_hi, ds_lo, g_hi, g_lo,
    far_part, far_y, far_sum, far_z, extra,
    wg_x, wg_xr, wg_y, wg_yr, wg_z, wg_zr, wg_q, wg_qr,
    dq_t, full_send, half_send, full_got, half_got,
    send_sem, recv_sem, local_sem,
):
    x = lax.axis_index("dp")
    s = lax.axis_index("seq")
    y = lax.div(s, 16)
    z = lax.rem(lax.div(s, 2), 8)
    c = lax.rem(s, 2)
    hz = lax.rem(z, 2)
    zz = lax.div(z, 2)
    t = lax.rem(s, 4)
    seg = lax.div(s, 4)
    xy = x * 4 + y

    def seat_of(d):
        core = c if d % 2 == 0 else 1 - c
        half = hz if d < 2 else 1 - hz
        return half * 2 + core

    def seg_peer(d):
        return (x, (y * 8 + zz * 2) * 2 + seat_of(d))

    def z_peer(j):
        return (x, (y * 8 + lax.rem(z + 2 * j, 8)) * 2 + c)

    def y_peer(j):
        return (x, (lax.rem(y + j, 4) * 8 + z) * 2 + c)

    def x_peer(j):
        return (lax.rem(x + j, 4), s)

    pushed = []

    def push(src, dst, device):
        i = len(pushed)
        copy = pltpu.make_async_remote_copy(
            src_ref=src, dst_ref=dst, send_sem=send_sem.at[i], recv_sem=recv_sem.at[i],
            device_id=device, device_id_type=MESH,
        )
        copy.start()
        pushed.append(copy)
        return copy

    def arrive(copies):
        for copy in copies:
            copy.wait_recv()

    loads = []
    for src, dst in (
        (w_in, w_seg.at[t]), (k_in, k_own), (v_in, v_own), (q_in, q_own), (g_in, g_seg.at[t]),
    ):
        copy = pltpu.make_async_copy(src, dst, local_sem.at[len(loads)])
        copy.start()
        loads.append(copy)

    barrier = pltpu.get_barrier_semaphore()
    for device in (
        [seg_peer(d) for d in (1, 2, 3)]
        + [z_peer(j) for j in (1, 2, 3)]
        + [y_peer(j) for j in (1, 2, 3)]
        + [x_peer(j) for j in (1, 2, 3)]
    ):
        pl.semaphore_signal(barrier, inc=1, device_id=device, device_id_type=MESH)
    pl.semaphore_wait(barrier, 12)

    loads[0].wait()
    w_moves = [push(w_seg.at[t], w_seg.at[t], seg_peer(d)) for d in (2, 3, 1)]

    def scatter_heads(own, send, seg_ref):
        for tt in range(SEATS):
            tile = 3 * (tt // 2) + 2 * (tt % 2)
            send[tt, 0:128, :] = own[:, tile * 128:(tile + 1) * 128]
            middle = 3 * (tt // 2) + 1
            top = own[0:64, middle * 128:(middle + 1) * 128]
            bottom = own[64:128, middle * 128:(middle + 1) * 128]
            if tt % 2 == 0:
                send[tt, 128:192, :] = jnp.where(low_lanes(top), top, flip(bottom))
            else:
                send[tt, 128:192, :] = jnp.where(low_lanes(top), flip(top), bottom)
        moves = [push(send.at[seat_of(d)], seg_ref.at[t], seg_peer(d)) for d in (2, 3, 1)]
        seg_ref[t] = send[t]
        return moves

    loads[1].wait()
    k_moves = scatter_heads(k_own, k_send, k_seg)
    loads[2].wait()
    v_moves = scatter_heads(v_own, v_send, v_seg)
    loads[3].wait()
    q_moves = scatter_heads(q_own, q_send, q_seg)
    loads[4].wait()
    g_rows = ROWS // G_CHUNKS
    g_across, g_beside = [], []
    for n in range(G_CHUNKS):
        part = g_seg.at[t, pl.ds(n * g_rows, g_rows)]
        g_across.append(push(part, part, seg_peer(2)))
    for n in range(G_CHUNKS):
        part = g_seg.at[t, pl.ds(n * g_rows, g_rows)]
        g_beside.append(push(part, part, seg_peer(1)))

    arrive(w_moves)
    full_tile = pl.multiple_of((3 * hz + 2 * c) * 128, 128)
    middle_tile = pl.multiple_of((3 * hz + 1) * 128, 128)
    for tt in range(SEATS):
        w_ring[zz, 3 * tt:3 * tt + 3, 0:128] = w_seg[tt, :, pl.ds(full_tile, 128)]
        middle = w_seg[tt, :, pl.ds(middle_tile, 128)]
        w_ring[zz, 3 * tt:3 * tt + 3, 128:256] = jnp.where(c == 1, flip(middle), middle)
    arrive([push(w_ring.at[zz], w_ring.at[zz], z_peer(j)) for j in (1, 2, 3)])
    for j in range(4):
        w_all[xy, 12 * j:12 * j + 12, :] = w_ring[j]
    arrive([push(w_all.at[xy], w_all.at[xy], y_peer(j)) for j in (1, 2, 3)])
    wx_moves = [
        push(w_all.at[pl.ds(x * 4, 4)], w_all.at[pl.ds(x * 4, 4)], x_peer(j)) for j in (1, 2, 3)
    ]

    arrive(k_moves)
    arrive(v_moves)
    first_head = 6 * hz + 4 * c
    heads = [first_head, first_head + 1, 6 * hz + 2 + c]
    offsets = [offset_ref[head] for head in heads]

    def long_rows(seg_ref, h):
        rows = []
        for r in range(8):
            if h < 2:
                rows.append(seg_ref[r // 2, pl.ds((r % 2) * 64 + offsets[h], 1), :])
            else:
                row = seg_ref[r // 2, pl.ds(128 + offsets[h], 1), :]
                rows.append(row if r % 2 == 0 else flip(row))
        return jnp.concatenate(rows, axis=0)

    for h in range(HEADS_HERE):
        key_rows, value_rows = long_rows(k_seg, h), long_rows(v_seg, h)
        low = low_lanes(key_rows)
        if h == 1:
            block = jnp.where(low, flip(key_rows), value_rows)
        else:
            block = jnp.where(low, key_rows, flip(value_rows))
        far[seg, 8 * h:8 * h + 8, :] = block
    far_moves = [push(far.at[seg], far.at[seg], z_peer(j)) for j in (1, 2, 3)]

    def head_blocks(seg_ref, tt):
        full = seg_ref[tt, 0:128, :]
        return ((0, full, False), (1, full, True), (2, unfold(seg_ref[tt, 128:192, :]), False))

    def as_keys(h, rows, block, upper, four, transposed):
        high, low = split(block)
        four[h, rows, 0:128] = twice(high, upper).astype(BF16)
        four[h, rows, 128:256] = twice(low, upper).astype(BF16)
        transposed[h, :, rows] = pair(block, upper).T.astype(BF16)

    for tt in range(SEATS):
        rows = slice(tt * 128, (tt + 1) * 128)
        for h, block, upper in head_blocks(k_seg, tt):
            as_keys(h, rows, block, upper, k4, kt)
        for h, block, upper in head_blocks(v_seg, tt):
            as_keys(h, rows, block, upper, v4, vt)

    arrive(far_moves)
    far_moves = [
        push(far.at[pl.ds(y * 4, 4)], far.at[pl.ds(y * 4, 4)], y_peer(j)) for j in (1, 2, 3)
    ]

    arrive(q_moves)
    for tt in range(SEATS):
        rows = slice(tt * 128, (tt + 1) * 128)
        for h, block, upper in head_blocks(q_seg, tt):
            both = pair(block * 0.125, upper).astype(BF16)
            q4[h, rows, 0:128] = both
            q4[h, rows, 128:256] = both

    arrive(far_moves)
    for h in range(HEADS_HERE):
        block = far[:, 8 * h:8 * h + 8, :].reshape(FAR, 128)
        as_keys(h, slice(SEG, KEYS), block, False, k4, kt)
        as_keys(h, slice(SEG, KEYS), block, True, v4, vt)

    valid = valid_ref[0]
    key_row = lax.broadcasted_iota(jnp.int32, (128, 256), 0)
    query_lane = lax.broadcasted_iota(jnp.int32, (128, 256), 1)

    def forward(h, carry):
        offset = offset_ref[jnp.where(h == 2, heads[2], first_head + h)]
        for qb in range(2):
            lanes = slice(qb * 256, (qb + 1) * 256)
            queries = q4[h, lanes, :]
            top = None
            for kb in range(5):
                rows = slice(kb * 128, (kb + 1) * 128)
                scores = dot_nt(k4[h, rows, :], queries)
                if kb < 4:
                    keep = (seg * SEG + kb * 128 + key_row < valid) | (
                        kb * 128 + key_row == qb * 256 + query_lane
                    )
                else:
                    keep = (key_row * SPACING + offset < valid) & (
                        lax.rem(query_lane, SPACING) == offset
                    )
                scores = jnp.where(keep, scores, MASKED)
                prob[h, rows, lanes] = scores
                here = jnp.max(scores, axis=0, keepdims=True)
                top = here if top is None else jnp.maximum(top, here)
            total = None
            for kb in range(5):
                rows = slice(kb * 128, (kb + 1) * 128)
                weight = jnp.exp(prob[h, rows, lanes] - top)
                prob[h, rows, lanes] = weight
                here = jnp.sum(weight, axis=0, keepdims=True)
                total = here if total is None else total + here
            scale = 1.0 / total
            for kb in range(5):
                rows = slice(kb * 128, (kb + 1) * 128)
                p = prob[h, rows, lanes] * scale
                prob[h, rows, lanes] = p
                high = p.astype(BF16)
                prob_hi[h, rows, lanes] = high
                prob_lo[h, rows, lanes] = (p - high.astype(F32)).astype(BF16)
            out = dot(vt[h], prob_hi[h, :, lanes]) + dot(vt[h], prob_lo[h, :, lanes])
            attn_t[h, :, lanes] = out[0:64] + out[64:128]
        return carry

    lax.fori_loop(0, HEADS_HERE, forward, 0)

    arrive(wx_moves)
    w_cols = w_all[...].reshape(WIDTH, 256)
    high = w_cols.astype(BF16)
    w_hi[...] = high
    w_lo[...] = (w_cols - high.astype(F32)).astype(BF16)
    forwarded = []
    for n in range(G_CHUNKS):
        g_across[n].wait_recv()
        part = g_seg.at[seat_of(2), pl.ds(n * g_rows, g_rows)]
        forwarded.append(push(part, part, seg_peer(1)))
    arrive(g_beside)
    arrive(forwarded)
    tile_row = lax.broadcasted_iota(jnp.int32, (ROWS, WIDTH), 0)
    for tt in range(SEATS):
        rows = slice(tt * 128, (tt + 1) * 128)
        grad = jnp.where(seg * SEG + tt * 128 + tile_row < valid, g_seg[tt], 0.0)
        high = grad.astype(BF16)
        low = (grad - high.astype(F32)).astype(BF16)
        g_hi[rows, :] = high
        g_lo[rows, :] = low
        out = dot(high, w_hi[...]) + dot(low, w_hi[...]) + dot(high, w_lo[...])
        full, middle = out[:, 0:128], out[:, 128:256]
        for h, block, upper in ((0, full, False), (1, full, True), (2, middle, False)):
            both = pair(block, upper).astype(BF16)
            do4[h, rows, 0:128] = both
            do4[h, rows, 128:256] = both
        turned = full.T
        do_t[0, :, rows] = turned[0:64]
        do_t[1, :, rows] = turned[64:128]
        do_t[2, :, rows] = middle.T[0:64]

    for h in range(HEADS_HERE):
        if h == 1:
            continue
        attn = attn_t[0:2].reshape(128, SEG) if h == 0 else attn_t[2]
        high = attn.astype(BF16)
        low = (attn - high.astype(F32)).astype(BF16)
        turned = dot(high, g_hi[...]) + dot(low, g_hi[...]) + dot(high, g_lo[...])
        if h == 2:
            turned = jnp.concatenate([turned, turned], axis=0)
        lanes = slice(0, 128) if h == 0 else slice(128, 256)
        for xx in range(X):
            wg_x[xx, :, lanes] = turned[:, xx * 192:(xx + 1) * 192].T
    wg_moves = [
        push(wg_x.at[lax.rem(x + j, 4)], wg_xr.at[j - 1], x_peer(j)) for j in (1, 2, 3)
    ]

    def score_grad(h, kb):
        rows = slice(kb * 128, (kb + 1) * 128)
        delta = jnp.sum(attn_t[h] * do_t[h], axis=0, keepdims=True)
        d_prob = dot_nt(v4[h, rows, :], do4[h])
        ds = prob[h, rows, :] * (d_prob - delta)
        high = ds.astype(BF16)
        ds_hi[h, rows, :] = high
        ds_lo[h, rows, :] = (ds - high.astype(F32)).astype(BF16)

    def key_value_grad(h, rows):
        queries, grads = q4[h, :, 0:128], do4[h, :, 0:128]
        d_key = dot(ds_hi[h, rows, :], queries) + dot(ds_lo[h, rows, :], queries)
        d_value = dot(prob_hi[h, rows, :], grads) + dot(prob_lo[h, rows, :], grads)
        return fold_halves(d_key), fold_halves(d_value)

    for h in range(HEADS_HERE):
        score_grad(h, 4)
        d_key, d_value = key_value_grad(h, slice(SEG, KEYS))
        block = jnp.where(low_lanes(d_key), d_key, d_value)
        far_part[:, 8 * h:8 * h + 8, :] = block.reshape(SEGMENTS, 8, 128)
    far_moves = [
        push(far_part.at[pl.ds(lax.rem(y + j, 4) * 4, 4)], far_y.at[j - 1], y_peer(j))
        for j in (1, 2, 3)
    ]

    def near(h):
        for kb in range(4):
            score_grad(h, kb)
        turned = dot(kt[h], ds_hi[h]) + dot(kt[h], ds_lo[h])
        dq_t[h] = (turned[0:64] + turned[64:128]) * 0.125
        return key_value_grad(h, slice(0, SEG))

    d_key, d_value = near(2)
    for tt in range(SEATS):
        block = dq_t[2, :, tt * 128:(tt + 1) * 128]
        block = jnp.concatenate([block, block], axis=0).T
        low = low_lanes(block[0:64])
        half_send[0, tt] = jnp.where(low, block[0:64], block[64:128])
        for n, part in ((1, d_key), (2, d_value)):
            top, bottom = part[tt * 128:tt * 128 + 64], part[tt * 128 + 64:tt * 128 + 128]
            half_send[n, tt] = jnp.where(low, top, bottom)
    out_moves = [
        push(half_send.at[:, seat_of(d)], half_got.at[:, t], seg_peer(d)) for d in (2, 3, 1)
    ]
    for n in range(3):
        half_got[n, t] = half_send[n, t]

    arrive(far_moves)
    far_sum[...] = far_part[pl.ds(y * 4, 4)] + far_y[0] + far_y[1] + far_y[2]
    far_moves = [push(far_sum.at[lax.rem(zz + j, 4)], far_z.at[j - 1], z_peer(j)) for j in (1, 2, 3)]

    low_key, low_value = near(0)
    high_key, high_value = near(1)
    lane_low = low_lanes(low_key)
    d_key = jnp.where(lane_low, low_key, high_key)
    d_value = jnp.where(lane_low, low_value, high_value)
    for tt in range(SEATS):
        rows = slice(tt * 128, (tt + 1) * 128)
        full_send[0, tt] = dq_t[0:2, :, rows].reshape(128, 128).T
        full_send[1, tt] = d_key[rows]
        full_send[2, tt] = d_value[rows]
    out_moves += [
        push(full_send.at[:, seat_of(d)], full_got.at[:, t], seg_peer(d)) for d in (2, 3, 1)
    ]
    for n in range(3):
        full_got[n, t] = full_send[n, t]

    arrive(far_moves)
    extra[t] = far_sum[zz] + far_z[0] + far_z[1] + far_z[2]
    extra_moves = [push(extra.at[t], extra.at[t], seg_peer(d)) for d in (2, 3, 1)]

    arrive(wg_moves)
    wg_sum = wg_x[x] + wg_xr[0] + wg_xr[1] + wg_xr[2]
    for yy in range(Y):
        wg_y[yy] = wg_sum[yy * 48:(yy + 1) * 48]
    arrive([push(wg_y.at[lax.rem(y + j, 4)], wg_yr.at[j - 1], y_peer(j)) for j in (1, 2, 3)])
    wg_sum = wg_y[y] + wg_yr[0] + wg_yr[1] + wg_yr[2]
    for j in range(4):
        wg_z[j] = wg_sum[j * 12:(j + 1) * 12]
    arrive([push(wg_z.at[lax.rem(zz + j, 4)], wg_zr.at[j - 1], z_peer(j)) for j in (1, 2, 3)])
    wg_sum = (wg_z[zz] + wg_zr[0] + wg_zr[1] + wg_zr[2]) * (8192.0 ** -0.5)
    for tt in range(SEATS):
        wg_q[tt] = wg_sum[tt * 3:(tt + 1) * 3]
    wg_moves = [push(wg_q.at[seat_of(d)], wg_qr.at[t], seg_peer(d)) for d in (2, 3, 1)]
    wg_qr[t] = wg_q[t]

    arrive(extra_moves)
    arrive(out_moves)
    row64 = lax.broadcasted_iota(jnp.int32, (64, 128), 0)
    low64 = lax.broadcasted_iota(jnp.int32, (64, 128), 1) < 64
    outs = (dq_out, dk_out, dv_out)

    def with_extra(n, r, tt, h, upper, block):
        if n == 0:
            return block
        head = 6 * (tt // 2) + (4 * (tt % 2) + h if h < 2 else 2 + tt % 2)
        row = extra[tt, pl.ds(8 * h + 2 * t + r, 1), :]
        if (n == 2) != upper:
            row = flip(row)
        keep = (row64 == offset_ref[head]) & (low64 != upper)
        return block + jnp.where(keep, jnp.broadcast_to(row, (64, 128)), 0.0)

    for n in range(3):
        for tt in range(SEATS):
            tile = 3 * (tt // 2) + 2 * (tt % 2)
            for r in range(2):
                block = full_got[n, tt, r * 64:(r + 1) * 64, :]
                block = with_extra(n, r, tt, 0, False, block)
                block = with_extra(n, r, tt, 1, True, block)
                outs[n][r * 64:(r + 1) * 64, tile * 128:(tile + 1) * 128] = block
        for half in range(2):
            tile = 3 * half + 1
            even, odd = half_got[n, 2 * half], half_got[n, 2 * half + 1]
            for r in range(2):
                if r == 0:
                    block = jnp.where(low64, even, flip(odd))
                else:
                    block = jnp.where(low64, flip(even), odd)
                block = with_extra(n, r, 2 * half, 2, False, block)
                block = with_extra(n, r, 2 * half + 1, 2, True, block)
                outs[n][r * 64:(r + 1) * 64, tile * 128:(tile + 1) * 128] = block

    arrive(wg_moves)
    for tt in range(SEATS):
        tile = 3 * (tt // 2) + 2 * (tt % 2)
        wg_out[:, tile * 128:(tile + 1) * 128] = wg_qr[tt, :, 0:128]
    for half in range(2):
        tile = 3 * half + 1
        even, odd = wg_qr[2 * half, :, 128:256], wg_qr[2 * half + 1, :, 128:256]
        wg_out[:, tile * 128:(tile + 1) * 128] = jnp.where(low_lanes(even), even, odd)

    for copy in pushed:
        copy.wait_send()


def on_device(queries, keys, values, out_grad, out_weight, valid_tiles, head_offsets):
    def block(*shape):
        return pltpu.VMEM(shape, F32)

    def half(*shape):
        return pltpu.VMEM(shape, BF16)

    scratch = [
        block(ROWS, WIDTH), block(ROWS, WIDTH), block(ROWS, WIDTH),
        block(4, 192, 128), block(4, 192, 128), block(4, 192, 128),
        block(4, 192, 128), block(4, 192, 128), block(4, 192, 128),
        block(4, ROWS, WIDTH),
        block(4, 3, WIDTH), block(4, 12, 256), block(16, 48, 256),
        half(WIDTH, 256), half(WIDTH, 256),
        block(SEGMENTS, 24, 128),
        half(3, SEG, 256), half(3, KEYS, 256), half(3, KEYS, 256),
        half(3, 128, KEYS), half(3, 128, KEYS),
        half(3, SEG, 256), block(3, 64, SEG), block(3, 64, SEG),
        block(3, KEYS, SEG), half(3, KEYS, SEG), half(3, KEYS, SEG),
        half(3, KEYS, SEG), half(3, KEYS, SEG),
        half(SEG, WIDTH), half(SEG, WIDTH),
        block(SEGMENTS, 24, 128), block(3, 4, 24, 128), block(4, 24, 128), block(3, 24, 128),
        block(4, 24, 128),
        block(4, 192, 256), block(3, 192, 256), block(4, 48, 256), block(3, 48, 256),
        block(4, 12, 256), block(3, 12, 256), block(4, 3, 256), block(4, 3, 256),
        block(3, 64, SEG),
        block(3, 4, 128, 128), block(3, 4, 64, 128), block(3, 4, 128, 128), block(3, 4, 64, 128),
        pltpu.SemaphoreType.DMA((SENDS,)), pltpu.SemaphoreType.DMA((SENDS,)),
        pltpu.SemaphoreType.DMA((5,)),
    ]
    whole = pl.BlockSpec(memory_space=pl.ANY)
    scalars = pl.BlockSpec(memory_space=pltpu.SMEM)
    vmem = pl.BlockSpec(memory_space=pltpu.VMEM)
    rows = jax.ShapeDtypeStruct((ROWS, WIDTH), F32)
    d_query, d_key, d_value, d_weight = pl.pallas_call(
        kernel,
        out_shape=(rows, rows, rows, jax.ShapeDtypeStruct((3, WIDTH), F32)),
        in_specs=[whole] * 5 + [scalars] * 2,
        out_specs=(vmem,) * 4,
        scratch_shapes=scratch,
        compiler_params=pltpu.CompilerParams(
            collective_id=0, has_side_effects=True, vmem_limit_bytes=52 * 1024 * 1024
        ),
        cost_estimate=pl.CostEstimate(
            flops=4_000_000_000, bytes_accessed=4_000_000, transcendentals=1_000_000
        ),
        name="dilated_backward",
    )(queries[0], keys[0], values[0], out_grad[0], out_weight, valid_tiles, head_offsets)
    return d_query[None], d_key[None], d_value[None], d_weight


def solution(mesh):
    from jax.sharding import PartitionSpec as P

    tiles = P("dp", "seq", None)
    weight = P(("dp", "seq"), None)
    return jax.shard_map(
        on_device,
        mesh=mesh,
        in_specs=(tiles, tiles, tiles, tiles, weight, P("dp"), P()),
        out_specs=(tiles, tiles, tiles, weight),
        check_vma=False,
    )
```

time: 694 us -> 92.7 us (0.13); the launches traced: 683 us -> 92.5 us
  waiting for transfers between devices: 410 us -> 0 us
  blocking collectives: 120 us -> 0 us
  Pallas kernels: 0 us -> 85 us
  matrix products: 62.3 us -> 0 us
  other arithmetic: 30.1 us -> 0 us
  local copies, waits for them, and re-layouts: 35.4 us -> 6.18 us
  between operations: 16.1 us -> 1.3 us
  starting transfers between devices: 9.9 us -> 0 us
    unnamed x5 -> x0, waiting for transfers between devices: 410 us -> none
    all_gather x2 -> x0, blocking collectives: 120 us -> none  [the longest x1 67.3 us: on_device(): lax.all_gather(dilated_value_rows, 'seq', axis=2, tiled=True)]
    pallas_call x0 -> x1, Pallas kernels: none -> 85 us  [on_device(): pl.pallas_call(kernel, out_shape=(rows, rows, rows, jax.ShapeDtypeStruct(...]
    dot_general x21 -> x0, matrix products: 62.3 us -> none  [the longest x19 51.9 us: elementwise_product(): jnp.einsum(form, left, right, precision=PRECISE, preferred_element_type=j...]
    select_n x9 -> x0, other arithmetic: 11 us -> none  [the longest x2 4.46 us: on_device(): jnp.where(upper, jnp.concatenate([other_value, value_group], 1), jnp.conc...]
    ppermute x8 -> x0, starting transfers between devices: 9.79 us -> none  [from_partner(): return lax.ppermute(block, axis, route)]
    another operation x9 -> x0, local copies, waits for them, and re-layouts: 9.34 us -> none
    unnamed x79 -> x12, local copies, waits for them, and re-layouts: 14.5 us -> 6.18 us
  transfers between devices with their start and end apart: 11 -> 0, of which waited for: 2 -> 0; matrix products, arithmetic and copies ran while one was open for 14% -> 0% of each run, Pallas kernels for 0% -> 0%
where the time goes in v1:
time: 92.7 us; the launch traced here: 92.5 us
  Pallas kernels  85 us (92%)
  local copies, waits for them, and re-layouts  6.18 us (7%)
  between operations  1.3 us (1%)
    pallas_call x1, Pallas kernels, on_device(): pl.pallas_call(kernel, out_shape=(rows, rows, rows, jax.ShapeDtypeStruct(...  85 us
    unnamed x12, local copies, waits for them, and re-layouts  6.18 us

profile of v1, /device:TPU:1, one launch (start us, length us, event | category | flops | bytes accessed | tf_op | source)
XLA Modules:
  0.0 92.5 jit_solution(4017331276787088410)
XLA Ops:
  1.3 0.0 copy-start.3
  1.3 0.6 copy-done.3
  1.9 0.0 copy-start
  1.9 1.0 %copy-done = f32[1,128,768]{2,1,0:T(8,128)S(1)} copy-done((f32[1,128,768]{2,1,0:T(8,128)S(1)}, f32[1,128,768]{2,1,0:T(8,128)}, u32[]{:S(2)}) %copy-start) | copy-done | bytes 393240
  2.9 0.0 copy-start.1
  2.9 1.0 %copy-done.1 = f32[1,128,768]{2,1,0:T(8,128)S(1)} copy-done((f32[1,128,768]{2,1,0:T(8,128)S(1)}, f32[1,128,768]{2,1,0:T(8,128)}, u32[]{:S(2)}) %copy-start.1) | copy-done | bytes 393240
  3.9 0.0 copy-start.2
  3.9 0.7 copy-done.2
  4.6 85.0 %dilated_backward.1 = (f32[128,768]{1,0:T(8,128)S(1)}, f32[128,768]{1,0:T(8,128)S(1)}, f32[128,768]{1,0:T(8,128)S(1)}, f32[3,768]{1,0:T(4,128)S(1)}) custom-call(f32[128,768]{1,0:T(8,128)S(1)} %bitcast.10, f32[128,768]{1,0:T(8,128)S(1)} %bitcast.11, f32[128,768]{1,0:T(8,128)} %bitcast.12, f32[128,768]{1,0:T(8,128)} %bitcast.13, f32[3,768]{1,0:T(4,128)S(1)} %copy-done.2, ...), custom_call_target="tpu_custom_call" | custom-call | flops 4000000000 | bytes 4000000 | tf_op jit(solution)/shard_map/dilated_backward/pallas_call | solution.py:514
  89.6 0.7 copy.16
  90.4 0.7 copy.17
  91.1 0.7 copy.18
  91.9 0.6 copy.19
Async XLA Ops:
  1.3 0.7 copy-start.3
  1.9 1.0 %copy-start = (f32[1,128,768]{2,1,0:T(8,128)S(1)}, f32[1,128,768]{2,1,0:T(8,128)}, u32[]{:S(2)}) copy-start(f32[1,128,768]{2,1,0:T(8,128)} %param.7) | copy-start | bytes 1179652
  2.9 1.0 %copy-start.1 = (f32[1,128,768]{2,1,0:T(8,128)S(1)}, f32[1,128,768]{2,1,0:T(8,128)}, u32[]{:S(2)}) copy-start(f32[1,128,768]{2,1,0:T(8,128)} %param.8) | copy-start | bytes 1179652
  3.9 0.7 copy-start.2

commit v2 on v1

v2 whole, which is shorter than its diff:
```python
import jax
import jax.numpy as jnp
from jax import lax
from jax.experimental import pallas as pl
from jax.experimental.pallas import tpu as pltpu

F32 = jnp.float32
BF16 = jnp.bfloat16
MASKED = -1e30
MESH = pl.DeviceIdType.MESH

X = 4
ROWS = 128
SEATS = 4
SEG = ROWS * SEATS
SPACING = 64
FAR = 128
WIDTH = 768
HEADS_HERE = 3
KEYS = SEG + FAR
G_CHUNKS = 4
G_EARLY = 2
FAR_FIRST = (8, 7, 9, 6, 10, 5, 11, 4, 12, 3, 13, 2, 14, 1, 15)
SENDS = 128


def dot(left, right):
    return lax.dot_general(left, right, (((1,), (0,)), ((), ())), preferred_element_type=F32)


def dot_nt(left, right):
    return lax.dot_general(left, right, (((1,), (1,)), ((), ())), preferred_element_type=F32)


def flip(block):
    return pltpu.roll(block, 64, 1)


def low_lanes(block):
    return lax.broadcasted_iota(jnp.int32, block.shape, 1) < 64


def split(block):
    high = block.astype(BF16).astype(F32)
    return high, block - high


def pair(block, upper):
    high, low = split(block)
    if upper:
        return jnp.where(low_lanes(block), flip(high), low)
    return jnp.where(low_lanes(block), high, flip(low))


def twice(block, upper):
    if upper:
        return jnp.where(low_lanes(block), flip(block), block)
    return jnp.where(low_lanes(block), block, flip(block))


def unfold(packed):
    return jnp.concatenate([packed, flip(packed)], axis=0)


def fold_halves(block):
    return block + flip(block)


def lanes_of(tile):
    return slice(tile * 128, (tile + 1) * 128)


def full_tile(seat):
    return 3 * (seat // 2) + 2 * (seat % 2)


def middle_tile(seat):
    return 3 * (seat // 2) + 1


def head_of(seat, h):
    return 6 * (seat // 2) + (2 + seat % 2 if h == 2 else 4 * (seat % 2) + h)


def kernel(
    q_in, k_in, v_in, g_in, w_in, valid_ref, offset_ref,
    full_got, half_got, last_got,
    q_own, k_own, v_own, w_own, half_in, half_seg, full_in, full_seg, g_seg,
    note, note_got, w_full, w_mid, w_hi, w_lo, far,
    q4, k4, v4, kt, vt, do4, do_t, attn_t, prob, prob_hi, prob_lo, ds_hi, ds_lo, g_hi, g_lo,
    far_part, far_got,
    wg_full, wg_full_1, wg_full_sum, wg_full_2, wg_mid, wg_mid_y, wg_mid_sum, wg_mid_x,
    last, dq_t, full_send, half_send,
    send_sem, recv_sem, local_sem,
):
    x = lax.axis_index("dp")
    s = lax.axis_index("seq")
    y = lax.div(s, 16)
    m = lax.rem(s, 16)
    z = lax.div(m, 2)
    c = lax.rem(s, 2)
    hz = lax.rem(z, 2)
    zz = lax.div(z, 2)
    t = lax.rem(s, 4)
    seg = lax.div(s, 4)

    def seat_of(d):
        core = c if d % 2 == 0 else 1 - c
        half = hz if d < 2 else 1 - hz
        return half * 2 + core

    def seg_peer(d):
        return (x, seg * 4 + seat_of(d))

    def ring_place(j):
        return lax.rem(m + j, 16)

    def ring_peer(j):
        return (x, y * 16 + ring_place(j))

    def y_place(j):
        return lax.rem(y + j, 4)

    def y_peer(j):
        return (x, y_place(j) * 16 + m)

    def x_place(j):
        return lax.rem(x + j, 4)

    def x_peer(j):
        return (x_place(j), s)

    pushed = []

    def push(src, dst, device):
        i = len(pushed)
        copy = pltpu.make_async_remote_copy(
            src_ref=src, dst_ref=dst, send_sem=send_sem.at[i], recv_sem=recv_sem.at[i],
            device_id=device, device_id_type=MESH,
        )
        copy.start()
        pushed.append(copy)
        return copy

    def arrive(copies):
        for copy in copies:
            copy.wait_recv()

    barrier = pltpu.get_barrier_semaphore()
    for device in (
        [ring_peer(j) for j in range(1, 16)]
        + [y_peer(j) for j in (1, 2, 3)]
        + [x_peer(j) for j in (1, 2, 3)]
    ):
        pl.semaphore_signal(barrier, inc=1, device_id=device, device_id_type=MESH)

    loads = []
    for src, dst in (
        (g_in, g_seg.at[t]), (k_in, k_own), (v_in, v_own), (w_in, w_own), (q_in, q_own),
    ):
        copy = pltpu.make_async_copy(src, dst, local_sem.at[len(loads)])
        copy.start()
        loads.append(copy)

    owns = (q_own, k_own, v_own)

    def deal(n):
        for tt in range(SEATS):
            full_in[tt, n] = owns[n][:, lanes_of(full_tile(tt))]
            top = owns[n][0:64, lanes_of(middle_tile(tt))]
            bottom = owns[n][64:128, lanes_of(middle_tile(tt))]
            if tt % 2 == 0:
                half_in[tt, n] = jnp.where(low_lanes(top), top, flip(bottom))
            else:
                half_in[tt, n] = jnp.where(low_lanes(top), flip(top), bottom)

    g_rows = ROWS // G_CHUNKS

    def g_part(seat, n):
        return g_seg.at[seat, pl.ds(n * g_rows, g_rows)]

    loads[0].wait()
    pl.semaphore_wait(barrier, 21)
    g_across = [push(g_part(t, n), g_part(t, n), seg_peer(2)) for n in range(G_EARLY)]

    loads[1].wait()
    deal(1)
    loads[2].wait()
    deal(2)

    def long_rows(tt, h, n):
        offset = offset_ref[head_of(tt, h)]
        if h == 2:
            row = half_in[tt, n, pl.ds(offset, 1), :]
            return jnp.concatenate([row, flip(row)], axis=0)
        return jnp.concatenate(
            [full_in[tt, n, pl.ds(r * 64 + offset, 1), :] for r in range(2)], axis=0
        )

    loads[3].wait()
    for tt in range(SEATS):
        note[tt, 0:3, :] = w_own[:, lanes_of(full_tile(tt))]
        note[tt, 3:6, :] = w_own[:, lanes_of(middle_tile(tt))]
        for h in range(HEADS_HERE):
            key_rows, value_rows = long_rows(tt, h, 1), long_rows(tt, h, 2)
            low = low_lanes(key_rows)
            if h == 1:
                rows = jnp.where(low, flip(key_rows), value_rows)
            else:
                rows = jnp.where(low, key_rows, flip(value_rows))
            note[tt, 6 + 2 * h:8 + 2 * h, :] = rows

    notes = [
        push(note.at[lax.rem(ring_place(j), 4)], note_got.at[m], ring_peer(j)) for j in FAR_FIRST
    ]
    g_across += [
        push(g_part(t, n), g_part(t, n), seg_peer(2)) for n in range(G_EARLY, G_CHUNKS)
    ]
    g_beside = [push(g_seg.at[t], g_seg.at[t], seg_peer(1))]
    note_got[m] = note[t]

    loads[4].wait()
    deal(0)
    half_seg[t] = half_in[t]
    full_seg[t] = full_in[t]

    arrive(notes)
    for mm in range(16):
        w_full[x, y, 3 * mm:3 * mm + 3, :] = note_got[mm, 0:3, :]
        w_mid[x, y, 3 * mm:3 * mm + 3, :] = note_got[mm, 3:6, :]
        for h in range(HEADS_HERE):
            far[y, h, 2 * mm:2 * mm + 2, :] = note_got[mm, 6 + 2 * h:8 + 2 * h, :]
    w_moves = [push(w_full.at[x, y], w_full.at[x, y], y_peer(j)) for j in (1, 3, 2)]
    w_moves += [push(w_mid.at[x, y], w_mid.at[x, y], x_peer(j)) for j in (1, 3, 2)]
    far_moves = [push(far.at[y], far.at[y], y_peer(j)) for j in (1, 3, 2)]
    half_moves = [push(half_in.at[seat_of(d)], half_seg.at[t], seg_peer(d)) for d in (2, 3, 1)]
    arrive(w_moves)
    w_moves = [push(w_full.at[x], w_full.at[x], x_peer(j)) for j in (1, 3, 2)]
    w_moves += [push(w_mid.at[:, y], w_mid.at[:, y], y_peer(j)) for j in (1, 3, 2)]
    arrive(far_moves)

    def as_keys(h, rows, block, upper, four, transposed):
        high, low = split(block)
        four[h, rows, 0:128] = twice(high, upper).astype(BF16)
        four[h, rows, 128:256] = twice(low, upper).astype(BF16)
        transposed[h, :, rows] = pair(block, upper).T.astype(BF16)

    for h in range(HEADS_HERE):
        block = far[:, h].reshape(FAR, 128)
        as_keys(h, slice(SEG, KEYS), block, False, k4, kt)
        as_keys(h, slice(SEG, KEYS), block, True, v4, vt)

    valid = valid_ref[0]
    tile_row = lax.broadcasted_iota(jnp.int32, (ROWS, WIDTH), 0)

    def take_grad(seat):
        rows = pl.ds(pl.multiple_of(seat * ROWS, ROWS), ROWS)
        grad = jnp.where(seg * SEG + seat * ROWS + tile_row < valid, g_seg[seat], 0.0)
        high = grad.astype(BF16)
        g_hi[rows, :] = high
        g_lo[rows, :] = (grad - high.astype(F32)).astype(BF16)

    take_grad(t)
    arrive(g_beside)
    take_grad(seat_of(1))
    g_forwarded = []
    for n in range(G_CHUNKS):
        g_across[n].wait_recv()
        g_forwarded.append(push(g_part(seat_of(2), n), g_part(seat_of(2), n), seg_peer(1)))
    full_moves = [
        push(full_in.at[seat_of(d), pl.ds(0, 2)], full_seg.at[t, pl.ds(0, 2)], seg_peer(d))
        for d in (2, 3, 1)
    ]
    full_value_moves = [
        push(full_in.at[seat_of(d), 2], full_seg.at[t, 2], seg_peer(d)) for d in (2, 3, 1)
    ]
    take_grad(seat_of(2))

    arrive(w_moves)
    for tile, ref in ((0, w_full), (1, w_mid)):
        columns = ref[...].reshape(WIDTH, 128)
        if tile == 1:
            columns = jnp.where(c == 1, flip(columns), columns)
        high = columns.astype(BF16)
        w_hi[:, lanes_of(tile)] = high
        w_lo[:, lanes_of(tile)] = (columns - high.astype(F32)).astype(BF16)

    arrive(g_forwarded)
    take_grad(seat_of(3))
    for tt in range(SEATS):
        rows = slice(tt * 128, (tt + 1) * 128)
        high, low = g_hi[rows, :], g_lo[rows, :]
        out = dot(high, w_hi[...]) + dot(low, w_hi[...]) + dot(high, w_lo[...])
        full, middle = out[:, 0:128], out[:, 128:256]
        for h, block, upper in ((0, full, False), (1, full, True), (2, middle, False)):
            both = pair(block, upper).astype(BF16)
            do4[h, rows, 0:128] = both
            do4[h, rows, 128:256] = both
        turned = full.T
        do_t[0, :, rows] = turned[0:64]
        do_t[1, :, rows] = turned[64:128]
        do_t[2, :, rows] = middle.T[0:64]

    def as_queries(h, rows, block, upper):
        both = pair(block * 0.125, upper).astype(BF16)
        q4[h, rows, 0:128] = both
        q4[h, rows, 128:256] = both

    key_row = lax.broadcasted_iota(jnp.int32, (128, 256), 0)
    query_lane = lax.broadcasted_iota(jnp.int32, (128, 256), 1)

    def weights(h):
        head = 6 * hz + jnp.where(h == 2, 2 + c, 4 * c + h)
        offset = offset_ref[head]
        for qb in range(2):
            lanes = slice(qb * 256, (qb + 1) * 256)
            queries = q4[h, lanes, :]
            top = None
            for kb in range(5):
                rows = slice(kb * 128, (kb + 1) * 128)
                scores = dot_nt(k4[h, rows, :], queries)
                if kb < 4:
                    keep = (seg * SEG + kb * 128 + key_row < valid) | (
                        kb * 128 + key_row == qb * 256 + query_lane
                    )
                else:
                    keep = (key_row * SPACING + offset < valid) & (
                        lax.rem(query_lane, SPACING) == offset
                    )
                scores = jnp.where(keep, scores, MASKED)
                prob[h, rows, lanes] = scores
                here = jnp.max(scores, axis=0, keepdims=True)
                top = here if top is None else jnp.maximum(top, here)
            total = None
            for kb in range(5):
                rows = slice(kb * 128, (kb + 1) * 128)
                weight = jnp.exp(prob[h, rows, lanes] - top)
                prob[h, rows, lanes] = weight
                here = jnp.sum(weight, axis=0, keepdims=True)
                total = here if total is None else total + here
            scale = 1.0 / total
            for kb in range(5):
                rows = slice(kb * 128, (kb + 1) * 128)
                p = prob[h, rows, lanes] * scale
                prob[h, rows, lanes] = p
                high = p.astype(BF16)
                prob_hi[h, rows, lanes] = high
                prob_lo[h, rows, lanes] = (p - high.astype(F32)).astype(BF16)

    def attention(h):
        for qb in range(2):
            lanes = slice(qb * 256, (qb + 1) * 256)
            out = dot(vt[h], prob_hi[h, :, lanes]) + dot(vt[h], prob_lo[h, :, lanes])
            attn_t[h, :, lanes] = out[0:64] + out[64:128]

    def value_grad(h):
        grads = do4[h, :, 0:128]
        return fold_halves(dot(prob_hi[h], grads) + dot(prob_lo[h], grads))

    def key_grad(h):
        queries = q4[h, :, 0:128]
        return fold_halves(dot(ds_hi[h], queries) + dot(ds_lo[h], queries))

    def score_grad(h):
        for qb in range(2):
            lanes = slice(qb * 256, (qb + 1) * 256)
            delta = jnp.sum(attn_t[h, :, lanes] * do_t[h, :, lanes], axis=0, keepdims=True)
            for kb in range(5):
                rows = slice(kb * 128, (kb + 1) * 128)
                d_prob = dot_nt(v4[h, rows, :], do4[h, lanes, :])
                ds = prob[h, rows, lanes] * (d_prob - delta)
                high = ds.astype(BF16)
                ds_hi[h, rows, lanes] = high
                ds_lo[h, rows, lanes] = (ds - high.astype(F32)).astype(BF16)

    def query_grad(h):
        turned = dot(kt[h], ds_hi[h]) + dot(kt[h], ds_lo[h])
        dq_t[h] = (turned[0:64] + turned[64:128]) * 0.125

    def weight_grad(attn):
        high = attn.astype(BF16)
        low = (attn - high.astype(F32)).astype(BF16)
        return dot(high, g_hi[...]) + dot(low, g_hi[...]) + dot(high, g_lo[...])

    def far_grad(h, d_key, d_value):
        d_key, d_value = d_key[SEG:KEYS], d_value[SEG:KEYS]
        block = jnp.where(low_lanes(d_key), d_key, d_value)
        far_part[:, h] = block.reshape(4, 32, 128)

    arrive(half_moves)
    for tt in range(SEATS):
        rows = slice(tt * 128, (tt + 1) * 128)
        as_queries(2, rows, unfold(half_seg[tt, 0]), False)
        as_keys(2, rows, unfold(half_seg[tt, 1]), False, k4, kt)
        as_keys(2, rows, unfold(half_seg[tt, 2]), False, v4, vt)
    weights(2)
    attention(2)
    turned = weight_grad(attn_t[2])
    turned = jnp.concatenate([turned, turned], axis=0)
    for xx in range(X):
        wg_mid[xx] = turned[:, xx * 192:(xx + 1) * 192].T.reshape(4, 48, 128)
    mid_moves = [push(wg_mid.at[:, y_place(j)], wg_mid_y.at[j - 1], y_peer(j)) for j in (1, 2, 3)]
    d_value = value_grad(2)
    score_grad(2)
    d_key = key_grad(2)
    query_grad(2)
    far_grad(2, d_key, d_value)
    for tt in range(SEATS):
        block = dq_t[2, :, tt * 128:(tt + 1) * 128]
        block = jnp.concatenate([block, block], axis=0).T
        low = low_lanes(block[0:64])
        half_send[tt, 0] = jnp.where(low, block[0:64], block[64:128])
        for n, part in ((1, d_key), (2, d_value)):
            top, bottom = part[tt * 128:tt * 128 + 64], part[tt * 128 + 64:tt * 128 + 128]
            half_send[tt, n] = jnp.where(low, top, bottom)
    half_out = [push(half_send.at[seat_of(d)], half_got.at[t], seg_peer(d)) for d in (2, 3, 1)]
    own_out = [pltpu.make_async_copy(half_send.at[t], half_got.at[t], local_sem.at[5])]
    own_out[0].start()
    far_moves = [
        push(far_part.at[y_place(j), pl.ds(2, 1)], far_got.at[j - 1, pl.ds(2, 1)], y_peer(j))
        for j in (1, 2, 3)
    ]
    arrive(mid_moves)
    wg_mid_sum[...] = wg_mid[:, y] + wg_mid_y[0] + wg_mid_y[1] + wg_mid_y[2]
    mid_moves = [push(wg_mid_sum.at[x_place(j)], wg_mid_x.at[j - 1], x_peer(j)) for j in (1, 2, 3)]

    arrive(full_moves)
    for tt in range(SEATS):
        rows = slice(tt * 128, (tt + 1) * 128)
        for h in range(2):
            as_queries(h, rows, full_seg[tt, 0], h == 1)
            as_keys(h, rows, full_seg[tt, 1], h == 1, k4, kt)
    weights(0)
    arrive(full_value_moves)
    for tt in range(SEATS):
        rows = slice(tt * 128, (tt + 1) * 128)
        for h in range(2):
            as_keys(h, rows, full_seg[tt, 2], h == 1, v4, vt)
    weights(1)
    attention(0)
    attention(1)
    turned = weight_grad(attn_t[0:2].reshape(128, SEG))
    for xx in range(X):
        block = turned[:, xx * 192:(xx + 1) * 192].T
        for yy in range(4):
            for n in range(2):
                wg_full[n, xx, yy] = block[yy * 48 + n * 24:yy * 48 + n * 24 + 24]
    wg_moves = [
        push(wg_full.at[0, x_place(j)], wg_full_1.at[0, j - 1], x_peer(j)) for j in (2, 1, 3)
    ] + [
        push(wg_full.at[1, :, y_place(j)], wg_full_1.at[1, j - 1], y_peer(j)) for j in (2, 1, 3)
    ]

    def send_full(n):
        moves = [push(full_send.at[seat_of(d), n], full_got.at[t, n], seg_peer(d)) for d in (2, 3, 1)]
        own_out.append(
            pltpu.make_async_copy(full_send.at[t, n], full_got.at[t, n], local_sem.at[6 + n])
        )
        own_out[-1].start()
        return moves

    def both_heads(low, high, n):
        block = jnp.where(low_lanes(low), low, high)
        for tt in range(SEATS):
            full_send[tt, n] = block[tt * 128:(tt + 1) * 128]
        return send_full(n)

    values_0, values_1 = value_grad(0), value_grad(1)
    full_out = both_heads(values_0, values_1, 2)
    score_grad(0)
    score_grad(1)
    keys_0, keys_1 = key_grad(0), key_grad(1)
    full_out += both_heads(keys_0, keys_1, 1)
    far_grad(0, keys_0, values_0)
    far_grad(1, keys_1, values_1)
    far_moves += [
        push(far_part.at[y_place(j), pl.ds(0, 2)], far_got.at[j - 1, pl.ds(0, 2)], y_peer(j))
        for j in (1, 2, 3)
    ]
    query_grad(0)
    query_grad(1)
    for tt in range(SEATS):
        full_send[tt, 0] = dq_t[0:2, :, tt * 128:(tt + 1) * 128].reshape(128, 128).T
    full_out += send_full(0)

    arrive(wg_moves)
    wg_full_sum[0] = wg_full[0, x] + wg_full_1[0, 0] + wg_full_1[0, 1] + wg_full_1[0, 2]
    wg_full_sum[1] = wg_full[1, :, y] + wg_full_1[1, 0] + wg_full_1[1, 1] + wg_full_1[1, 2]
    wg_moves = [
        push(wg_full_sum.at[0, y_place(j)], wg_full_2.at[0, j - 1], y_peer(j)) for j in (2, 1, 3)
    ] + [
        push(wg_full_sum.at[1, x_place(j)], wg_full_2.at[1, j - 1], x_peer(j)) for j in (2, 1, 3)
    ]
    arrive(mid_moves)
    mid_rows = wg_mid_sum[x] + wg_mid_x[0] + wg_mid_x[1] + wg_mid_x[2]
    for mm in range(16):
        last[mm, 3:6, :] = mid_rows[3 * mm:3 * mm + 3]
    arrive(far_moves)
    for h in range(HEADS_HERE):
        rows = far_part[y, h] + far_got[0, h] + far_got[1, h] + far_got[2, h]
        for mm in range(16):
            last[mm, 6 + 2 * h:8 + 2 * h, :] = rows[2 * mm:2 * mm + 2]
    arrive(wg_moves)
    rows_0 = wg_full_sum[0, y] + wg_full_2[0, 0] + wg_full_2[0, 1] + wg_full_2[0, 2]
    rows_1 = wg_full_sum[1, x] + wg_full_2[1, 0] + wg_full_2[1, 1] + wg_full_2[1, 2]
    for mm in range(16):
        rows = rows_0 if mm < 8 else rows_1
        last[mm, 0:3, :] = rows[3 * (mm % 8):3 * (mm % 8) + 3]
    last_moves = [
        push(last.at[ring_place(j)], last_got.at[m], ring_peer(j)) for j in FAR_FIRST
    ]
    own_out.append(pltpu.make_async_copy(last.at[m], last_got.at[m], local_sem.at[9]))
    own_out[-1].start()

    arrive(half_out)
    arrive(full_out)
    arrive(last_moves)
    for copy in own_out:
        copy.wait()
    for copy in pushed:
        copy.wait_send()


def put_together(
    full_in, half_in, last_in, offset_ref, dq_out, dk_out, dv_out, wg_out,
    full_got, half_got, last_got, dq_own, dk_own, dv_own, wg_own, in_sem, out_sem,
):
    loads = []
    for n in range(3):
        for src, dst in ((full_in, full_got), (half_in, half_got)):
            loads.append(
                pltpu.make_async_copy(src.at[:, n], dst.at[:, n], in_sem.at[len(loads)])
            )
    loads.append(pltpu.make_async_copy(last_in, last_got, in_sem.at[6]))
    for copy in loads:
        copy.start()
    stores = [
        pltpu.make_async_copy(src, dst, out_sem.at[n])
        for n, (src, dst) in enumerate(
            ((dq_own, dq_out), (dk_own, dk_out), (dv_own, dv_out), (wg_own, wg_out))
        )
    ]
    row64 = lax.broadcasted_iota(jnp.int32, (64, 128), 0)
    low64 = lax.broadcasted_iota(jnp.int32, (64, 128), 1) < 64
    outs = (dq_own, dk_own, dv_own)
    notes = []

    def with_extra(n, r, tt, h, upper, block):
        if n == 0:
            return block
        row = notes[tt][6 + 2 * h + r:7 + 2 * h + r]
        if (n == 2) != upper:
            row = flip(row)
        keep = (row64 == offset_ref[head_of(tt, h)]) & (low64 != upper)
        return block + jnp.where(keep, jnp.broadcast_to(row, (64, 128)), 0.0)

    for n in range(3):
        loads[2 * n].wait()
        loads[2 * n + 1].wait()
        if n == 1:
            loads[6].wait()
            notes += [
                last_got[tt] + last_got[4 + tt] + last_got[8 + tt] + last_got[12 + tt]
                for tt in range(SEATS)
            ]
        for half in range(2):
            even, odd = half_got[2 * half, n], half_got[2 * half + 1, n]
            for r in range(2):
                if r == 0:
                    block = jnp.where(low64, even, flip(odd))
                else:
                    block = jnp.where(low64, flip(even), odd)
                block = with_extra(n, r, 2 * half, 2, False, block)
                block = with_extra(n, r, 2 * half + 1, 2, True, block)
                outs[n][r * 64:(r + 1) * 64, lanes_of(3 * half + 1)] = block
        for tt in range(SEATS):
            for r in range(2):
                block = full_got[tt, n, r * 64:(r + 1) * 64, :]
                block = with_extra(n, r, tt, 0, False, block)
                block = with_extra(n, r, tt, 1, True, block)
                outs[n][r * 64:(r + 1) * 64, lanes_of(full_tile(tt))] = block
        stores[n].start()

    scale = 8192.0 ** -0.5
    for tt in range(SEATS):
        wg_own[:, lanes_of(full_tile(tt))] = notes[tt][0:3] * scale
    for half in range(2):
        even, odd = notes[2 * half][3:6], notes[2 * half + 1][3:6]
        wg_own[:, lanes_of(3 * half + 1)] = jnp.where(low_lanes(even), even, odd) * scale
    stores[3].start()
    for copy in stores:
        copy.wait()


def on_device(queries, keys, values, out_grad, out_weight, valid_tiles, head_offsets):
    def block(*shape):
        return pltpu.VMEM(shape, F32)

    def half(*shape):
        return pltpu.VMEM(shape, BF16)

    scratch = [
        block(ROWS, WIDTH), block(ROWS, WIDTH), block(ROWS, WIDTH), block(3, WIDTH),
        block(4, 3, 64, 128), block(4, 3, 64, 128), block(4, 3, 128, 128), block(4, 3, 128, 128),
        block(4, ROWS, WIDTH),
        block(4, 12, 128), block(16, 12, 128),
        block(4, 4, 48, 128), block(4, 4, 48, 128), half(WIDTH, 256), half(WIDTH, 256),
        block(4, 3, 32, 128),
        half(3, SEG, 256), half(3, KEYS, 256), half(3, KEYS, 256),
        half(3, 128, KEYS), half(3, 128, KEYS),
        half(3, SEG, 256), block(3, 64, SEG), block(3, 64, SEG),
        block(3, KEYS, SEG), half(3, KEYS, SEG), half(3, KEYS, SEG),
        half(3, KEYS, SEG), half(3, KEYS, SEG),
        half(SEG, WIDTH), half(SEG, WIDTH),
        block(4, 3, 32, 128), block(3, 3, 32, 128),
        block(2, 4, 4, 24, 128), block(2, 3, 4, 24, 128), block(2, 4, 24, 128), block(2, 3, 24, 128),
        block(4, 4, 48, 128), block(3, 4, 48, 128), block(4, 48, 128), block(3, 48, 128),
        block(16, 12, 128), block(3, 64, SEG),
        block(4, 3, 128, 128), block(4, 3, 64, 128),
        pltpu.SemaphoreType.DMA((SENDS,)), pltpu.SemaphoreType.DMA((SENDS,)),
        pltpu.SemaphoreType.DMA((10,)),
    ]
    whole = pl.BlockSpec(memory_space=pltpu.HBM)
    scalars = pl.BlockSpec(memory_space=pltpu.SMEM)
    rows = jax.ShapeDtypeStruct((ROWS, WIDTH), F32)
    got = pl.pallas_call(
        kernel,
        out_shape=(
            jax.ShapeDtypeStruct((4, 3, 128, 128), F32),
            jax.ShapeDtypeStruct((4, 3, 64, 128), F32),
            jax.ShapeDtypeStruct((16, 12, 128), F32),
        ),
        in_specs=[whole] * 5 + [scalars] * 2,
        out_specs=(whole,) * 3,
        scratch_shapes=scratch,
        compiler_params=pltpu.CompilerParams(
            collective_id=0, has_side_effects=True, vmem_limit_bytes=60 * 1024 * 1024
        ),
        cost_estimate=pl.CostEstimate(
            flops=4_000_000_000, bytes_accessed=4_000_000, transcendentals=1_000_000
        ),
        name="dilated_backward",
    )(queries[0], keys[0], values[0], out_grad[0], out_weight, valid_tiles, head_offsets)
    d_query, d_key, d_value, d_weight = pl.pallas_call(
        put_together,
        out_shape=(rows, rows, rows, jax.ShapeDtypeStruct((3, WIDTH), F32)),
        in_specs=[whole] * 3 + [scalars],
        out_specs=(whole,) * 4,
        scratch_shapes=[
            block(4, 3, 128, 128), block(4, 3, 64, 128), block(16, 12, 128),
            block(ROWS, WIDTH), block(ROWS, WIDTH), block(ROWS, WIDTH), block(3, WIDTH),
            pltpu.SemaphoreType.DMA((7,)), pltpu.SemaphoreType.DMA((4,)),
        ],
        compiler_params=pltpu.CompilerParams(vmem_limit_bytes=60 * 1024 * 1024),
        cost_estimate=pl.CostEstimate(flops=1_000_000, bytes_accessed=2_500_000, transcendentals=0),
        name="put_together",
    )(*got, head_offsets)
    return d_query[None], d_key[None], d_value[None], d_weight


def solution(mesh):
    from jax.sharding import PartitionSpec as P

    tiles = P("dp", "seq", None)
    weight = P(("dp", "seq"), None)
    return jax.shard_map(
        on_device,
        mesh=mesh,
        in_specs=(tiles, tiles, tiles, tiles, weight, P("dp"), P()),
        out_specs=(tiles, tiles, tiles, weight),
        check_vma=False,
    )
```

time: 92.7 us -> 64.8 us (0.70)
  Pallas kernels: 85 us -> 63.4 us
  local copies, waits for them, and re-layouts: 6.18 us -> 0 us
    pallas_call x1 -> x2, Pallas kernels: 85 us -> 63.4 us  [the longest x1 60.3 us: on_device(): pl.pallas_call(kernel, out_shape=(jax.ShapeDtypeStruct((4, 3, 128, 128),...]
    unnamed x12 -> x0, local copies, waits for them, and re-layouts: 6.18 us -> none
where the time goes in v2:
time: 64.8 us; the launch traced here: 64.7 us
  Pallas kernels  63.4 us (98%)
  between operations  1.29 us (2%)
    pallas_call x1, Pallas kernels, on_device(): pl.pallas_call(kernel, out_shape=(jax.ShapeDtypeStruct((4, 3, 128, 128),...  60.3 us
    pallas_call x1, Pallas kernels, on_device(): pl.pallas_call(put_together, out_shape=(rows, rows, rows, jax.ShapeDtypeS...  3.09 us

profile of v2, /device:TPU:1, one launch (start us, length us, event | category | flops | bytes accessed | tf_op | source)
XLA Modules:
  0.0 64.7 jit_solution(2375290685104428245)
XLA Ops:
  1.3 60.3 %dilated_backward.1 = (f32[4,3,128,128]{3,2,1,0:T(8,128)}, f32[4,3,64,128]{3,2,1,0:T(8,128)}, f32[16,12,128]{2,1,0:T(8,128)}) custom-call(f32[128,768]{1,0:T(8,128)} %bitcast.7, f32[128,768]{1,0:T(8,128)} %bitcast.8, f32[128,768]{1,0:T(8,128)} %bitcast.9, f32[128,768]{1,0:T(8,128)} %bitcast.10, f32[3,768]{1,0:T(4,128)} %w_in.1, s32[1]{0:T(128)S(6)} %copy.11.valid_ref, ...), custom_call_target="tpu_custom_call" | custom-call | flops 4000000000 | bytes 4000000 | tf_op jit(solution)/shard_map/dilated_backward/pallas_call | solution.py:626
  61.6 3.1 %put_together.1 = (f32[128,768]{1,0:T(8,128)}, f32[128,768]{1,0:T(8,128)}, f32[128,768]{1,0:T(8,128)}, f32[3,768]{1,0:T(4,128)}) custom-call(f32[4,3,128,128]{3,2,1,0:T(8,128)} %get-tuple-element.11.full_in, f32[4,3,64,128]{3,2,1,0:T(8,128)} %get-tuple-element.12.half_in, f32[16,12,128]{2,1,0:T(8,128)} %get-tuple-element.13.last_in, s32[12]{0:T(128)} %offset_ref.3), custom_call_target="tpu_custom_call" | custom-call | flops 1000000 | bytes 2500000 | tf_op jit(solution)/shard_map/put_together/pallas_call | solution.py:644

commit v3 on v2

--- a/solution.py
+++ b/solution.py
@@ -21,7 +21,7 @@
 G_CHUNKS = 4
 G_EARLY = 2
 FAR_FIRST = (8, 7, 9, 6, 10, 5, 11, 4, 12, 3, 13, 2, 14, 1, 15)
-SENDS = 128
+SENDS = 32
 
 
 def dot(left, right):
@@ -89,7 +89,7 @@
     note, note_got, w_full, w_mid, w_hi, w_lo, far,
     q4, k4, v4, kt, vt, do4, do_t, attn_t, prob, prob_hi, prob_lo, ds_hi, ds_lo, g_hi, g_lo,
     far_part, far_got,
-    wg_full, wg_full_1, wg_full_sum, wg_full_2, wg_mid, wg_mid_y, wg_mid_sum, wg_mid_x,
+    wg_full, wg_full_1, wg_full_sum, wg_full_2, wg_mid, wg_mid_1, wg_mid_sum, wg_mid_2,
     last, dq_t, full_send, half_send,
     send_sem, recv_sem, local_sem,
 ):
@@ -130,21 +130,29 @@
     def x_peer(j):
         return (x_place(j), s)
 
-    pushed = []
-
-    def push(src, dst, device):
-        i = len(pushed)
-        copy = pltpu.make_async_remote_copy(
-            src_ref=src, dst_ref=dst, send_sem=send_sem.at[i], recv_sem=recv_sem.at[i],
-            device_id=device, device_id_type=MESH,
-        )
-        copy.start()
-        pushed.append(copy)
-        return copy
-
-    def arrive(copies):
-        for copy in copies:
-            copy.wait_recv()
+    class Group:
+        count = 0
+
+        def __init__(self, like, copies=()):
+            self.like, self.index = like, Group.count
+            Group.count += 1
+            self.add(copies)
+
+        def describe(self, src, dst, device):
+            return pltpu.make_async_remote_copy(
+                src_ref=src, dst_ref=dst, send_sem=send_sem.at[self.index],
+                recv_sem=recv_sem.at[self.index], device_id=device, device_id_type=MESH,
+            )
+
+        def add(self, copies):
+            for src, dst, device in copies:
+                self.describe(src, dst, device).start()
+
+        def arrive(self):
+            self.describe(self.like, self.like, seg_peer(1)).wait_recv()
+
+        def sent(self):
+            self.describe(self.like, self.like, seg_peer(1)).wait_send()
 
     barrier = pltpu.get_barrier_semaphore()
     for device in (
@@ -181,7 +189,10 @@
 
     loads[0].wait()
     pl.semaphore_wait(barrier, 21)
-    g_across = [push(g_part(t, n), g_part(t, n), seg_peer(2)) for n in range(G_EARLY)]
+    def send_across(n):
+        return Group(g_part(0, n), [(g_part(t, n), g_part(t, n), seg_peer(2))])
+
+    g_across = [send_across(n) for n in range(G_EARLY)]
 
     loads[1].wait()
     deal(1)
@@ -210,34 +221,55 @@
                 rows = jnp.where(low, key_rows, flip(value_rows))
             note[tt, 6 + 2 * h:8 + 2 * h, :] = rows
 
-    notes = [
-        push(note.at[lax.rem(ring_place(j), 4)], note_got.at[m], ring_peer(j)) for j in FAR_FIRST
-    ]
-    g_across += [
-        push(g_part(t, n), g_part(t, n), seg_peer(2)) for n in range(G_EARLY, G_CHUNKS)
-    ]
-    g_beside = [push(g_seg.at[t], g_seg.at[t], seg_peer(1))]
+    notes = Group(
+        note_got.at[pl.ds(0, 15)],
+        [(note.at[lax.rem(ring_place(j), 4)], note_got.at[m], ring_peer(j)) for j in FAR_FIRST],
+    )
+    g_across += [send_across(n) for n in range(G_EARLY, G_CHUNKS)]
     note_got[m] = note[t]
-
     loads[4].wait()
     deal(0)
+    full_in_moves = Group(
+        full_seg.at[pl.ds(0, 3), pl.ds(0, 2)],
+        [
+            (full_in.at[seat_of(d), pl.ds(0, 2)], full_seg.at[t, pl.ds(0, 2)], seg_peer(d))
+            for d in (2, 3, 1)
+        ],
+    )
+    value_in_moves = Group(
+        full_seg.at[pl.ds(0, 3), 2],
+        [(full_in.at[seat_of(d), 2], full_seg.at[t, 2], seg_peer(d)) for d in (2, 3, 1)],
+    )
+    g_beside = Group(g_seg.at[0], [(g_seg.at[t], g_seg.at[t], seg_peer(1))])
+    half_in_moves = Group(
+        half_seg.at[pl.ds(0, 3)],
+        [(half_in.at[seat_of(d)], half_seg.at[t], seg_peer(d)) for d in (2, 3, 1)],
+    )
     half_seg[t] = half_in[t]
     full_seg[t] = full_in[t]
 
-    arrive(notes)
+    notes.arrive()
     for mm in range(16):
         w_full[x, y, 3 * mm:3 * mm + 3, :] = note_got[mm, 0:3, :]
         w_mid[x, y, 3 * mm:3 * mm + 3, :] = note_got[mm, 3:6, :]
         for h in range(HEADS_HERE):
             far[y, h, 2 * mm:2 * mm + 2, :] = note_got[mm, 6 + 2 * h:8 + 2 * h, :]
-    w_moves = [push(w_full.at[x, y], w_full.at[x, y], y_peer(j)) for j in (1, 3, 2)]
-    w_moves += [push(w_mid.at[x, y], w_mid.at[x, y], x_peer(j)) for j in (1, 3, 2)]
-    far_moves = [push(far.at[y], far.at[y], y_peer(j)) for j in (1, 3, 2)]
-    half_moves = [push(half_in.at[seat_of(d)], half_seg.at[t], seg_peer(d)) for d in (2, 3, 1)]
-    arrive(w_moves)
-    w_moves = [push(w_full.at[x], w_full.at[x], x_peer(j)) for j in (1, 3, 2)]
-    w_moves += [push(w_mid.at[:, y], w_mid.at[:, y], y_peer(j)) for j in (1, 3, 2)]
-    arrive(far_moves)
+    w_first = Group(
+        w_full.at[pl.ds(0, 2), pl.ds(0, 3)],
+        [(w_full.at[x, y], w_full.at[x, y], y_peer(j)) for j in (2, 1, 3)]
+        + [(w_mid.at[x, y], w_mid.at[x, y], x_peer(j)) for j in (2, 1, 3)],
+    )
+    far_moves = Group(
+        far.at[pl.ds(0, 3)], [(far.at[y], far.at[y], y_peer(j)) for j in (2, 1, 3)]
+    )
+    w_first.arrive()
+    w_full_moves = Group(
+        w_full.at[pl.ds(0, 3)], [(w_full.at[x], w_full.at[x], x_peer(j)) for j in (2, 1, 3)]
+    )
+    w_mid_moves = Group(
+        w_mid.at[pl.ds(0, 3)], [(w_mid.at[:, y], w_mid.at[:, y], y_peer(j)) for j in (2, 1, 3)]
+    )
+    far_moves.arrive()
 
     def as_keys(h, rows, block, upper, four, transposed):
         high, low = split(block)
@@ -261,22 +293,17 @@
         g_lo[rows, :] = (grad - high.astype(F32)).astype(BF16)
 
     take_grad(t)
-    arrive(g_beside)
+    g_beside.arrive()
     take_grad(seat_of(1))
-    g_forwarded = []
+    g_forwarded = Group(g_seg.at[0])
     for n in range(G_CHUNKS):
-        g_across[n].wait_recv()
-        g_forwarded.append(push(g_part(seat_of(2), n), g_part(seat_of(2), n), seg_peer(1)))
-    full_moves = [
-        push(full_in.at[seat_of(d), pl.ds(0, 2)], full_seg.at[t, pl.ds(0, 2)], seg_peer(d))
-        for d in (2, 3, 1)
-    ]
-    full_value_moves = [
-        push(full_in.at[seat_of(d), 2], full_seg.at[t, 2], seg_peer(d)) for d in (2, 3, 1)
-    ]
+        g_across[n].arrive()
+        part = g_part(seat_of(2), n)
+        g_forwarded.add([(part, part, seg_peer(1))])
     take_grad(seat_of(2))
 
-    arrive(w_moves)
+    w_full_moves.arrive()
+    w_mid_moves.arrive()
     for tile, ref in ((0, w_full), (1, w_mid)):
         columns = ref[...].reshape(WIDTH, 128)
         if tile == 1:
@@ -285,7 +312,7 @@
         w_hi[:, lanes_of(tile)] = high
         w_lo[:, lanes_of(tile)] = (columns - high.astype(F32)).astype(BF16)
 
-    arrive(g_forwarded)
+    g_forwarded.arrive()
     take_grad(seat_of(3))
     for tt in range(SEATS):
         rows = slice(tt * 128, (tt + 1) * 128)
@@ -387,7 +414,77 @@
         block = jnp.where(low_lanes(d_key), d_key, d_value)
         far_part[:, h] = block.reshape(4, 32, 128)
 
-    arrive(half_moves)
+    for group in [notes, w_first, far_moves, g_beside] + g_across:
+        group.sent()
+    full_in_moves.arrive()
+    for tt in range(SEATS):
+        rows = slice(tt * 128, (tt + 1) * 128)
+        for h in range(2):
+            as_queries(h, rows, full_seg[tt, 0], h == 1)
+            as_keys(h, rows, full_seg[tt, 1], h == 1, k4, kt)
+    weights(0)
+    weights(1)
+    value_in_moves.arrive()
+    for tt in range(SEATS):
+        rows = slice(tt * 128, (tt + 1) * 128)
+        for h in range(2):
+            as_keys(h, rows, full_seg[tt, 2], h == 1, v4, vt)
+    attention(0)
+    attention(1)
+    turned = weight_grad(attn_t[0:2].reshape(128, SEG))
+    for xx in range(X):
+        block = turned[:, xx * 192:(xx + 1) * 192].T
+        for yy in range(4):
+            for n in range(2):
+                wg_full[n, xx, yy] = block[yy * 48 + n * 24:yy * 48 + n * 24 + 24]
+    wg_first = Group(
+        wg_full_1,
+        [(wg_full.at[0, x_place(j)], wg_full_1.at[0, j - 1], x_peer(j)) for j in (2, 1, 3)]
+        + [(wg_full.at[1, :, y_place(j)], wg_full_1.at[1, j - 1], y_peer(j)) for j in (2, 1, 3)],
+    )
+
+    full_out = Group(full_got.at[pl.ds(0, 3)])
+    own_out = []
+
+    def keep_own(src, dst):
+        copy = pltpu.make_async_copy(src, dst, local_sem.at[5 + len(own_out)])
+        copy.start()
+        own_out.append(copy)
+
+    def send_full(n):
+        full_out.add(
+            (full_send.at[seat_of(d), n], full_got.at[t, n], seg_peer(d)) for d in (2, 3, 1)
+        )
+        keep_own(full_send.at[t, n], full_got.at[t, n])
+
+    def both_heads(low, high, n):
+        block = jnp.where(low_lanes(low), low, high)
+        for tt in range(SEATS):
+            full_send[tt, n] = block[tt * 128:(tt + 1) * 128]
+        send_full(n)
+
+    values_0, values_1 = value_grad(0), value_grad(1)
+    both_heads(values_0, values_1, 2)
+    score_grad(0)
+    score_grad(1)
+    keys_0, keys_1 = key_grad(0), key_grad(1)
+    both_heads(keys_0, keys_1, 1)
+    far_grad(0, keys_0, values_0)
+    far_grad(1, keys_1, values_1)
+    far_out = Group(
+        far_got,
+        [
+            (far_part.at[y_place(j), pl.ds(0, 2)], far_got.at[j - 1, pl.ds(0, 2)], y_peer(j))
+            for j in (2, 1, 3)
+        ],
+    )
+    query_grad(0)
+    query_grad(1)
+    for tt in range(SEATS):
+        full_send[tt, 0] = dq_t[0:2, :, tt * 128:(tt + 1) * 128].reshape(128, 128).T
+    send_full(0)
+
+    half_in_moves.arrive()
     for tt in range(SEATS):
         rows = slice(tt * 128, (tt + 1) * 128)
         as_queries(2, rows, unfold(half_seg[tt, 0]), False)
@@ -398,13 +495,30 @@
     turned = weight_grad(attn_t[2])
     turned = jnp.concatenate([turned, turned], axis=0)
     for xx in range(X):
-        wg_mid[xx] = turned[:, xx * 192:(xx + 1) * 192].T.reshape(4, 48, 128)
-    mid_moves = [push(wg_mid.at[:, y_place(j)], wg_mid_y.at[j - 1], y_peer(j)) for j in (1, 2, 3)]
+        block = turned[:, xx * 192:(xx + 1) * 192].T
+        for yy in range(4):
+            top, bottom = block[yy * 48:yy * 48 + 24], block[yy * 48 + 24:yy * 48 + 48]
+            wg_mid[xx, yy] = jnp.where(low_lanes(top), top, bottom)
+    mid_first = Group(
+        wg_mid_1, [(wg_mid.at[x_place(j)], wg_mid_1.at[j - 1], x_peer(j)) for j in (2, 1, 3)]
+    )
+    wg_first.arrive()
+    wg_full_sum[0] = wg_full[0, x] + wg_full_1[0, 0] + wg_full_1[0, 1] + wg_full_1[0, 2]
+    wg_full_sum[1] = wg_full[1, :, y] + wg_full_1[1, 0] + wg_full_1[1, 1] + wg_full_1[1, 2]
+    wg_second = Group(
+        wg_full_2,
+        [(wg_full_sum.at[0, y_place(j)], wg_full_2.at[0, j - 1], y_peer(j)) for j in (2, 1, 3)]
+        + [(wg_full_sum.at[1, x_place(j)], wg_full_2.at[1, j - 1], x_peer(j)) for j in (2, 1, 3)],
+    )
     d_value = value_grad(2)
     score_grad(2)
     d_key = key_grad(2)
+    far_grad(2, d_key, d_value)
+    far_out.add(
+        (far_part.at[y_place(j), pl.ds(2, 1)], far_got.at[j - 1, pl.ds(2, 1)], y_peer(j))
+        for j in (2, 1, 3)
+    )
     query_grad(2)
-    far_grad(2, d_key, d_value)
     for tt in range(SEATS):
         block = dq_t[2, :, tt * 128:(tt + 1) * 128]
         block = jnp.concatenate([block, block], axis=0).T
@@ -413,112 +527,49 @@
         for n, part in ((1, d_key), (2, d_value)):
             top, bottom = part[tt * 128:tt * 128 + 64], part[tt * 128 + 64:tt * 128 + 128]
             half_send[tt, n] = jnp.where(low, top, bottom)
-    half_out = [push(half_send.at[seat_of(d)], half_got.at[t], seg_peer(d)) for d in (2, 3, 1)]
-    own_out = [pltpu.make_async_copy(half_send.at[t], half_got.at[t], local_sem.at[5])]
-    own_out[0].start()
-    far_moves = [
-        push(far_part.at[y_place(j), pl.ds(2, 1)], far_got.at[j - 1, pl.ds(2, 1)], y_peer(j))
-        for j in (1, 2, 3)
-    ]
-    arrive(mid_moves)
-    wg_mid_sum[...] = wg_mid[:, y] + wg_mid_y[0] + wg_mid_y[1] + wg_mid_y[2]
-    mid_moves = [push(wg_mid_sum.at[x_place(j)], wg_mid_x.at[j - 1], x_peer(j)) for j in (1, 2, 3)]
-
-    arrive(full_moves)
-    for tt in range(SEATS):
-        rows = slice(tt * 128, (tt + 1) * 128)
-        for h in range(2):
-            as_queries(h, rows, full_seg[tt, 0], h == 1)
-            as_keys(h, rows, full_seg[tt, 1], h == 1, k4, kt)
-    weights(0)
-    arrive(full_value_moves)
-    for tt in range(SEATS):
-        rows = slice(tt * 128, (tt + 1) * 128)
-        for h in range(2):
-            as_keys(h, rows, full_seg[tt, 2], h == 1, v4, vt)
-    weights(1)
-    attention(0)
-    attention(1)
-    turned = weight_grad(attn_t[0:2].reshape(128, SEG))
-    for xx in range(X):
-        block = turned[:, xx * 192:(xx + 1) * 192].T
-        for yy in range(4):
-            for n in range(2):
-                wg_full[n, xx, yy] = block[yy * 48 + n * 24:yy * 48 + n * 24 + 24]
-    wg_moves = [
-        push(wg_full.at[0, x_place(j)], wg_full_1.at[0, j - 1], x_peer(j)) for j in (2, 1, 3)
-    ] + [
-        push(wg_full.at[1, :, y_place(j)], wg_full_1.at[1, j - 1], y_peer(j)) for j in (2, 1, 3)
-    ]
-
-    def send_full(n):
-        moves = [push(full_send.at[seat_of(d), n], full_got.at[t, n], seg_peer(d)) for d in (2, 3, 1)]
-        own_out.append(
-            pltpu.make_async_copy(full_send.at[t, n], full_got.at[t, n], local_sem.at[6 + n])
-        )
-        own_out[-1].start()
-        return moves
-
-    def both_heads(low, high, n):
-        block = jnp.where(low_lanes(low), low, high)
-        for tt in range(SEATS):
-            full_send[tt, n] = block[tt * 128:(tt + 1) * 128]
-        return send_full(n)
-
-    values_0, values_1 = value_grad(0), value_grad(1)
-    full_out = both_heads(values_0, values_1, 2)
-    score_grad(0)
-    score_grad(1)
-    keys_0, keys_1 = key_grad(0), key_grad(1)
-    full_out += both_heads(keys_0, keys_1, 1)
-    far_grad(0, keys_0, values_0)
-    far_grad(1, keys_1, values_1)
-    far_moves += [
-        push(far_part.at[y_place(j), pl.ds(0, 2)], far_got.at[j - 1, pl.ds(0, 2)], y_peer(j))
-        for j in (1, 2, 3)
-    ]
-    query_grad(0)
-    query_grad(1)
-    for tt in range(SEATS):
-        full_send[tt, 0] = dq_t[0:2, :, tt * 128:(tt + 1) * 128].reshape(128, 128).T
-    full_out += send_full(0)
-
-    arrive(wg_moves)
-    wg_full_sum[0] = wg_full[0, x] + wg_full_1[0, 0] + wg_full_1[0, 1] + wg_full_1[0, 2]
-    wg_full_sum[1] = wg_full[1, :, y] + wg_full_1[1, 0] + wg_full_1[1, 1] + wg_full_1[1, 2]
-    wg_moves = [
-        push(wg_full_sum.at[0, y_place(j)], wg_full_2.at[0, j - 1], y_peer(j)) for j in (2, 1, 3)
-    ] + [
-        push(wg_full_sum.at[1, x_place(j)], wg_full_2.at[1, j - 1], x_peer(j)) for j in (2, 1, 3)
-    ]
-    arrive(mid_moves)
-    mid_rows = wg_mid_sum[x] + wg_mid_x[0] + wg_mid_x[1] + wg_mid_x[2]
-    for mm in range(16):
-        last[mm, 3:6, :] = mid_rows[3 * mm:3 * mm + 3]
-    arrive(far_moves)
-    for h in range(HEADS_HERE):
-        rows = far_part[y, h] + far_got[0, h] + far_got[1, h] + far_got[2, h]
-        for mm in range(16):
-            last[mm, 6 + 2 * h:8 + 2 * h, :] = rows[2 * mm:2 * mm + 2]
-    arrive(wg_moves)
+    half_out = Group(
+        half_got.at[pl.ds(0, 3)],
+        [(half_send.at[seat_of(d)], half_got.at[t], seg_peer(d)) for d in (2, 3, 1)],
+    )
+    keep_own(half_send.at[t], half_got.at[t])
+
+    mid_first.arrive()
+    wg_mid_sum[...] = wg_mid[x] + wg_mid_1[0] + wg_mid_1[1] + wg_mid_1[2]
+    mid_second = Group(
+        wg_mid_2, [(wg_mid_sum.at[y_place(j)], wg_mid_2.at[j - 1], y_peer(j)) for j in (2, 1, 3)]
+    )
+    wg_second.arrive()
     rows_0 = wg_full_sum[0, y] + wg_full_2[0, 0] + wg_full_2[0, 1] + wg_full_2[0, 2]
     rows_1 = wg_full_sum[1, x] + wg_full_2[1, 0] + wg_full_2[1, 1] + wg_full_2[1, 2]
     for mm in range(16):
         rows = rows_0 if mm < 8 else rows_1
         last[mm, 0:3, :] = rows[3 * (mm % 8):3 * (mm % 8) + 3]
-    last_moves = [
-        push(last.at[ring_place(j)], last_got.at[m], ring_peer(j)) for j in FAR_FIRST
-    ]
-    own_out.append(pltpu.make_async_copy(last.at[m], last_got.at[m], local_sem.at[9]))
-    own_out[-1].start()
-
-    arrive(half_out)
-    arrive(full_out)
-    arrive(last_moves)
+    far_out.arrive()
+    for h in range(HEADS_HERE):
+        rows = far_part[y, h] + far_got[0, h] + far_got[1, h] + far_got[2, h]
+        for mm in range(16):
+            last[mm, 6 + 2 * h:8 + 2 * h, :] = rows[2 * mm:2 * mm + 2]
+    mid_second.arrive()
+    packed = wg_mid_sum[y] + wg_mid_2[0] + wg_mid_2[1] + wg_mid_2[2]
+    for mm in range(16):
+        rows = packed if mm < 8 else flip(packed)
+        last[mm, 3:6, :] = rows[3 * (mm % 8):3 * (mm % 8) + 3]
+    last_moves = Group(
+        last_got.at[pl.ds(0, 15)],
+        [(last.at[ring_place(j)], last_got.at[m], ring_peer(j)) for j in FAR_FIRST],
+    )
+    keep_own(last.at[m], last_got.at[m])
+
+    for group in (
+        w_full_moves, w_mid_moves, g_forwarded, full_in_moves, value_in_moves, half_in_moves,
+        wg_first, mid_first, wg_second, far_out, mid_second,
+    ):
+        group.sent()
     for copy in own_out:
         copy.wait()
-    for copy in pushed:
-        copy.wait_send()
+    for group in (full_out, half_out, last_moves):
+        group.arrive()
+        group.sent()
 
 
 def put_together(
@@ -586,7 +637,7 @@
         wg_own[:, lanes_of(full_tile(tt))] = notes[tt][0:3] * scale
     for half in range(2):
         even, odd = notes[2 * half][3:6], notes[2 * half + 1][3:6]
-        wg_own[:, lanes_of(3 * half + 1)] = jnp.where(low_lanes(even), even, odd) * scale
+        wg_own[:, lanes_of(3 * half + 1)] = jnp.where(low_lanes(even), even, flip(odd)) * scale
     stores[3].start()
     for copy in stores:
         copy.wait()
@@ -614,7 +665,7 @@
         half(SEG, WIDTH), half(SEG, WIDTH),
         block(4, 3, 32, 128), block(3, 3, 32, 128),
         block(2, 4, 4, 24, 128), block(2, 3, 4, 24, 128), block(2, 4, 24, 128), block(2, 3, 24, 128),
-        block(4, 4, 48, 128), block(3, 4, 48, 128), block(4, 48, 128), block(3, 48, 128),
+        block(4, 4, 24, 128), block(3, 4, 24, 128), block(4, 24, 128), block(3, 24, 128),
         block(16, 12, 128), block(3, 64, SEG),
         block(4, 3, 128, 128), block(4, 3, 64, 128),
         pltpu.SemaphoreType.DMA((SENDS,)), pltpu.SemaphoreType.DMA((SENDS,)),

time: 64.8 us -> 60.2 us (0.929)
  Pallas kernels: 63.4 us -> 58.7 us
    pallas_call x1, Pallas kernels: 60.3 us -> 55.6 us  [on_device(): pl.pallas_call(kernel, out_shape=(jax.ShapeDtypeStruct((4, 3, 128, 128),...]
where the time goes in v3:
time: 60.2 us; the launch traced here: 60 us
  Pallas kernels  58.7 us (98%)
  between operations  1.29 us (2%)
    pallas_call x1, Pallas kernels, on_device(): pl.pallas_call(kernel, out_shape=(jax.ShapeDtypeStruct((4, 3, 128, 128),...  55.6 us
    pallas_call x1, Pallas kernels, on_device(): pl.pallas_call(put_together, out_shape=(rows, rows, rows, jax.ShapeDtypeS...  3.1 us

profile of v3, /device:TPU:1, one launch (start us, length us, event | category | flops | bytes accessed | tf_op | source)
XLA Modules:
  0.0 60.0 jit_solution(17961699732059815253)
XLA Ops:
  1.3 55.6 %dilated_backward.1 = (f32[4,3,128,128]{3,2,1,0:T(8,128)}, f32[4,3,64,128]{3,2,1,0:T(8,128)}, f32[16,12,128]{2,1,0:T(8,128)}) custom-call(f32[128,768]{1,0:T(8,128)} %bitcast.7, f32[128,768]{1,0:T(8,128)} %bitcast.8, f32[128,768]{1,0:T(8,128)} %bitcast.9, f32[128,768]{1,0:T(8,128)} %bitcast.10, f32[3,768]{1,0:T(4,128)} %w_in.1, s32[1]{0:T(128)S(6)} %copy.11.valid_ref, ...), custom_call_target="tpu_custom_call" | custom-call | flops 4000000000 | bytes 4000000 | tf_op jit(solution)/shard_map/dilated_backward/pallas_call | solution.py:677
  56.9 3.1 %put_together.1 = (f32[128,768]{1,0:T(8,128)}, f32[128,768]{1,0:T(8,128)}, f32[128,768]{1,0:T(8,128)}, f32[3,768]{1,0:T(4,128)}) custom-call(f32[4,3,128,128]{3,2,1,0:T(8,128)} %get-tuple-element.11.full_in, f32[4,3,64,128]{3,2,1,0:T(8,128)} %get-tuple-element.12.half_in, f32[16,12,128]{2,1,0:T(8,128)} %get-tuple-element.13.last_in, s32[12]{0:T(128)} %offset_ref.3), custom_call_target="tpu_custom_call" | custom-call | flops 1000000 | bytes 2500000 | tf_op jit(solution)/shard_map/put_together/pallas_call | solution.py:695

commit v4 on v3

--- a/solution.py
+++ b/solution.py
@@ -84,13 +84,13 @@
 
 def kernel(
     q_in, k_in, v_in, g_in, w_in, valid_ref, offset_ref,
-    full_got, half_got, last_got,
+    full_got, half_got, last_got, far_note_got,
     q_own, k_own, v_own, w_own, half_in, half_seg, full_in, full_seg, g_seg,
     note, note_got, w_full, w_mid, w_hi, w_lo, far,
     q4, k4, v4, kt, vt, do4, do_t, attn_t, prob, prob_hi, prob_lo, ds_hi, ds_lo, g_hi, g_lo,
     far_part, far_got,
     wg_full, wg_full_1, wg_full_sum, wg_full_2, wg_mid, wg_mid_1, wg_mid_sum, wg_mid_2,
-    last, dq_t, full_send, half_send,
+    last, far_note, dq_t, full_send, half_send,
     send_sem, recv_sem, local_sem,
 ):
     x = lax.axis_index("dp")
@@ -154,6 +154,14 @@
         def sent(self):
             self.describe(self.like, self.like, seg_peer(1)).wait_send()
 
+    loads = []
+    for src, dst in (
+        (g_in, g_seg.at[t]), (k_in, k_own), (v_in, v_own), (w_in, w_own), (q_in, q_own),
+    ):
+        copy = pltpu.make_async_copy(src, dst, local_sem.at[len(loads)])
+        copy.start()
+        loads.append(copy)
+
     barrier = pltpu.get_barrier_semaphore()
     for device in (
         [ring_peer(j) for j in range(1, 16)]
@@ -161,14 +169,6 @@
         + [x_peer(j) for j in (1, 2, 3)]
     ):
         pl.semaphore_signal(barrier, inc=1, device_id=device, device_id_type=MESH)
-
-    loads = []
-    for src, dst in (
-        (g_in, g_seg.at[t]), (k_in, k_own), (v_in, v_own), (w_in, w_own), (q_in, q_own),
-    ):
-        copy = pltpu.make_async_copy(src, dst, local_sem.at[len(loads)])
-        copy.start()
-        loads.append(copy)
 
     owns = (q_own, k_own, v_own)
 
@@ -242,8 +242,15 @@
     )
     g_beside = Group(g_seg.at[0], [(g_seg.at[t], g_seg.at[t], seg_peer(1))])
     half_in_moves = Group(
-        half_seg.at[pl.ds(0, 3)],
-        [(half_in.at[seat_of(d)], half_seg.at[t], seg_peer(d)) for d in (2, 3, 1)],
+        half_seg.at[pl.ds(0, 3), pl.ds(0, 2)],
+        [
+            (half_in.at[seat_of(d), pl.ds(0, 2)], half_seg.at[t, pl.ds(0, 2)], seg_peer(d))
+            for d in (2, 3, 1)
+        ],
+    )
+    half_value_moves = Group(
+        half_seg.at[pl.ds(0, 3), 2],
+        [(half_in.at[seat_of(d), 2], half_seg.at[t, 2], seg_peer(d)) for d in (2, 3, 1)],
     )
     half_seg[t] = half_in[t]
     full_seg[t] = full_in[t]
@@ -414,6 +421,28 @@
         block = jnp.where(low_lanes(d_key), d_key, d_value)
         far_part[:, h] = block.reshape(4, 32, 128)
 
+    def sum_first(parts, got):
+        return Group(
+            got,
+            [(parts.at[0, x_place(j)], got.at[0, j - 1], x_peer(j)) for j in (2, 1, 3)]
+            + [(parts.at[1, :, y_place(j)], got.at[1, j - 1], y_peer(j)) for j in (2, 1, 3)],
+        )
+
+    def sum_second(parts, got, sums, got_next):
+        sums[0] = parts[0, x] + got[0, 0] + got[0, 1] + got[0, 2]
+        sums[1] = parts[1, :, y] + got[1, 0] + got[1, 1] + got[1, 2]
+        return Group(
+            got_next,
+            [(sums.at[0, y_place(j)], got_next.at[0, j - 1], y_peer(j)) for j in (2, 1, 3)]
+            + [(sums.at[1, x_place(j)], got_next.at[1, j - 1], x_peer(j)) for j in (2, 1, 3)],
+        )
+
+    def sum_last(sums, got_next):
+        return (
+            sums[0, y] + got_next[0, 0] + got_next[0, 1] + got_next[0, 2],
+            sums[1, x] + got_next[1, 0] + got_next[1, 1] + got_next[1, 2],
+        )
+
     for group in [notes, w_first, far_moves, g_beside] + g_across:
         group.sent()
     full_in_moves.arrive()
@@ -437,11 +466,7 @@
         for yy in range(4):
             for n in range(2):
                 wg_full[n, xx, yy] = block[yy * 48 + n * 24:yy * 48 + n * 24 + 24]
-    wg_first = Group(
-        wg_full_1,
-        [(wg_full.at[0, x_place(j)], wg_full_1.at[0, j - 1], x_peer(j)) for j in (2, 1, 3)]
-        + [(wg_full.at[1, :, y_place(j)], wg_full_1.at[1, j - 1], y_peer(j)) for j in (2, 1, 3)],
-    )
+    wg_first = sum_first(wg_full, wg_full_1)
 
     full_out = Group(full_got.at[pl.ds(0, 3)])
     own_out = []
@@ -478,19 +503,17 @@
             for j in (2, 1, 3)
         ],
     )
-    query_grad(0)
-    query_grad(1)
-    for tt in range(SEATS):
-        full_send[tt, 0] = dq_t[0:2, :, tt * 128:(tt + 1) * 128].reshape(128, 128).T
-    send_full(0)
 
     half_in_moves.arrive()
     for tt in range(SEATS):
         rows = slice(tt * 128, (tt + 1) * 128)
         as_queries(2, rows, unfold(half_seg[tt, 0]), False)
         as_keys(2, rows, unfold(half_seg[tt, 1]), False, k4, kt)
+    weights(2)
+    half_value_moves.arrive()
+    for tt in range(SEATS):
+        rows = slice(tt * 128, (tt + 1) * 128)
         as_keys(2, rows, unfold(half_seg[tt, 2]), False, v4, vt)
-    weights(2)
     attention(2)
     turned = weight_grad(attn_t[2])
     turned = jnp.concatenate([turned, turned], axis=0)
@@ -498,18 +521,18 @@
         block = turned[:, xx * 192:(xx + 1) * 192].T
         for yy in range(4):
             top, bottom = block[yy * 48:yy * 48 + 24], block[yy * 48 + 24:yy * 48 + 48]
-            wg_mid[xx, yy] = jnp.where(low_lanes(top), top, bottom)
-    mid_first = Group(
-        wg_mid_1, [(wg_mid.at[x_place(j)], wg_mid_1.at[j - 1], x_peer(j)) for j in (2, 1, 3)]
-    )
+            packed = jnp.where(low_lanes(top), top, bottom)
+            wg_mid[0, xx, yy] = packed[0:12]
+            wg_mid[1, xx, yy] = packed[12:24]
+
+    mid_first = sum_first(wg_mid, wg_mid_1)
+    query_grad(0)
+    query_grad(1)
+    for tt in range(SEATS):
+        full_send[tt, 0] = dq_t[0:2, :, tt * 128:(tt + 1) * 128].reshape(128, 128).T
+    send_full(0)
     wg_first.arrive()
-    wg_full_sum[0] = wg_full[0, x] + wg_full_1[0, 0] + wg_full_1[0, 1] + wg_full_1[0, 2]
-    wg_full_sum[1] = wg_full[1, :, y] + wg_full_1[1, 0] + wg_full_1[1, 1] + wg_full_1[1, 2]
-    wg_second = Group(
-        wg_full_2,
-        [(wg_full_sum.at[0, y_place(j)], wg_full_2.at[0, j - 1], y_peer(j)) for j in (2, 1, 3)]
-        + [(wg_full_sum.at[1, x_place(j)], wg_full_2.at[1, j - 1], x_peer(j)) for j in (2, 1, 3)],
-    )
+    wg_second = sum_second(wg_full, wg_full_1, wg_full_sum, wg_full_2)
     d_value = value_grad(2)
     score_grad(2)
     d_key = key_grad(2)
@@ -518,6 +541,8 @@
         (far_part.at[y_place(j), pl.ds(2, 1)], far_got.at[j - 1, pl.ds(2, 1)], y_peer(j))
         for j in (2, 1, 3)
     )
+    mid_first.arrive()
+    mid_second = sum_second(wg_mid, wg_mid_1, wg_mid_sum, wg_mid_2)
     query_grad(2)
     for tt in range(SEATS):
         block = dq_t[2, :, tt * 128:(tt + 1) * 128]
@@ -527,64 +552,54 @@
         for n, part in ((1, d_key), (2, d_value)):
             top, bottom = part[tt * 128:tt * 128 + 64], part[tt * 128 + 64:tt * 128 + 128]
             half_send[tt, n] = jnp.where(low, top, bottom)
-    half_out = Group(
-        half_got.at[pl.ds(0, 3)],
-        [(half_send.at[seat_of(d)], half_got.at[t], seg_peer(d)) for d in (2, 3, 1)],
-    )
-    keep_own(half_send.at[t], half_got.at[t])
-
-    mid_first.arrive()
-    wg_mid_sum[...] = wg_mid[x] + wg_mid_1[0] + wg_mid_1[1] + wg_mid_1[2]
-    mid_second = Group(
-        wg_mid_2, [(wg_mid_sum.at[y_place(j)], wg_mid_2.at[j - 1], y_peer(j)) for j in (2, 1, 3)]
-    )
+
+    def to_owners(notes, got):
+        return Group(
+            got.at[pl.ds(0, 15)],
+            [(notes.at[ring_place(j)], got.at[m], ring_peer(j)) for j in FAR_FIRST],
+        )
+
     wg_second.arrive()
-    rows_0 = wg_full_sum[0, y] + wg_full_2[0, 0] + wg_full_2[0, 1] + wg_full_2[0, 2]
-    rows_1 = wg_full_sum[1, x] + wg_full_2[1, 0] + wg_full_2[1, 1] + wg_full_2[1, 2]
+    parts = sum_last(wg_full_sum, wg_full_2)
     for mm in range(16):
-        rows = rows_0 if mm < 8 else rows_1
-        last[mm, 0:3, :] = rows[3 * (mm % 8):3 * (mm % 8) + 3]
+        last[mm, 0:3, :] = parts[mm // 8][3 * (mm % 8):3 * (mm % 8) + 3]
     far_out.arrive()
     for h in range(HEADS_HERE):
         rows = far_part[y, h] + far_got[0, h] + far_got[1, h] + far_got[2, h]
         for mm in range(16):
-            last[mm, 6 + 2 * h:8 + 2 * h, :] = rows[2 * mm:2 * mm + 2]
+            far_note[mm, 2 * h:2 * h + 2, :] = rows[2 * mm:2 * mm + 2]
+    far_last = to_owners(far_note, far_note_got)
     mid_second.arrive()
-    packed = wg_mid_sum[y] + wg_mid_2[0] + wg_mid_2[1] + wg_mid_2[2]
+    parts = sum_last(wg_mid_sum, wg_mid_2)
     for mm in range(16):
-        rows = packed if mm < 8 else flip(packed)
-        last[mm, 3:6, :] = rows[3 * (mm % 8):3 * (mm % 8) + 3]
-    last_moves = Group(
-        last_got.at[pl.ds(0, 15)],
-        [(last.at[ring_place(j)], last_got.at[m], ring_peer(j)) for j in FAR_FIRST],
-    )
+        rows = parts[mm // 4 % 2]
+        last[mm, 3:6, :] = (rows if mm < 8 else flip(rows))[3 * (mm % 4):3 * (mm % 4) + 3]
+    last_moves = to_owners(last, last_got)
+    half_out = Group(
+        half_got.at[pl.ds(0, 3)],
+        [(half_send.at[seat_of(d)], half_got.at[t], seg_peer(d)) for d in (2, 3, 1)],
+    )
+    keep_own(half_send.at[t], half_got.at[t])
     keep_own(last.at[m], last_got.at[m])
+    keep_own(far_note.at[m], far_note_got.at[m])
 
     for group in (
         w_full_moves, w_mid_moves, g_forwarded, full_in_moves, value_in_moves, half_in_moves,
-        wg_first, mid_first, wg_second, far_out, mid_second,
+        half_value_moves, wg_first, mid_first, wg_second, far_out, mid_second, full_out,
     ):
         group.sent()
+    full_out.arrive()
     for copy in own_out:
         copy.wait()
-    for group in (full_out, half_out, last_moves):
+    for group in (far_last, last_moves, half_out):
+        group.sent()
         group.arrive()
-        group.sent()
 
 
 def put_together(
-    full_in, half_in, last_in, offset_ref, dq_out, dk_out, dv_out, wg_out,
-    full_got, half_got, last_got, dq_own, dk_own, dv_own, wg_own, in_sem, out_sem,
+    full_got, half_got, last_got, far_got, offset_ref, dq_out, dk_out, dv_out, wg_out,
+    dq_own, dk_own, dv_own, wg_own, out_sem,
 ):
-    loads = []
-    for n in range(3):
-        for src, dst in ((full_in, full_got), (half_in, half_got)):
-            loads.append(
-                pltpu.make_async_copy(src.at[:, n], dst.at[:, n], in_sem.at[len(loads)])
-            )
-    loads.append(pltpu.make_async_copy(last_in, last_got, in_sem.at[6]))
-    for copy in loads:
-        copy.start()
     stores = [
         pltpu.make_async_copy(src, dst, out_sem.at[n])
         for n, (src, dst) in enumerate(
@@ -594,26 +609,21 @@
     row64 = lax.broadcasted_iota(jnp.int32, (64, 128), 0)
     low64 = lax.broadcasted_iota(jnp.int32, (64, 128), 1) < 64
     outs = (dq_own, dk_own, dv_own)
-    notes = []
+    far_rows, wg_rows = [
+        [got[tt] + got[4 + tt] + got[8 + tt] + got[12 + tt] for tt in range(SEATS)]
+        for got in (far_got, last_got)
+    ]
 
     def with_extra(n, r, tt, h, upper, block):
         if n == 0:
             return block
-        row = notes[tt][6 + 2 * h + r:7 + 2 * h + r]
+        row = far_rows[tt][2 * h + r:2 * h + r + 1]
         if (n == 2) != upper:
             row = flip(row)
         keep = (row64 == offset_ref[head_of(tt, h)]) & (low64 != upper)
         return block + jnp.where(keep, jnp.broadcast_to(row, (64, 128)), 0.0)
 
     for n in range(3):
-        loads[2 * n].wait()
-        loads[2 * n + 1].wait()
-        if n == 1:
-            loads[6].wait()
-            notes += [
-                last_got[tt] + last_got[4 + tt] + last_got[8 + tt] + last_got[12 + tt]
-                for tt in range(SEATS)
-            ]
         for half in range(2):
             even, odd = half_got[2 * half, n], half_got[2 * half + 1, n]
             for r in range(2):
@@ -634,9 +644,9 @@
 
     scale = 8192.0 ** -0.5
     for tt in range(SEATS):
-        wg_own[:, lanes_of(full_tile(tt))] = notes[tt][0:3] * scale
+        wg_own[:, lanes_of(full_tile(tt))] = wg_rows[tt][0:3] * scale
     for half in range(2):
-        even, odd = notes[2 * half][3:6], notes[2 * half + 1][3:6]
+        even, odd = wg_rows[2 * half][3:6], wg_rows[2 * half + 1][3:6]
         wg_own[:, lanes_of(3 * half + 1)] = jnp.where(low_lanes(even), even, flip(odd)) * scale
     stores[3].start()
     for copy in stores:
@@ -665,44 +675,49 @@
         half(SEG, WIDTH), half(SEG, WIDTH),
         block(4, 3, 32, 128), block(3, 3, 32, 128),
         block(2, 4, 4, 24, 128), block(2, 3, 4, 24, 128), block(2, 4, 24, 128), block(2, 3, 24, 128),
-        block(4, 4, 24, 128), block(3, 4, 24, 128), block(4, 24, 128), block(3, 24, 128),
-        block(16, 12, 128), block(3, 64, SEG),
+        block(2, 4, 4, 12, 128), block(2, 3, 4, 12, 128), block(2, 4, 12, 128), block(2, 3, 12, 128),
+        block(16, 6, 128), block(16, 6, 128), block(3, 64, SEG),
         block(4, 3, 128, 128), block(4, 3, 64, 128),
         pltpu.SemaphoreType.DMA((SENDS,)), pltpu.SemaphoreType.DMA((SENDS,)),
-        pltpu.SemaphoreType.DMA((10,)),
+        pltpu.SemaphoreType.DMA((11,)),
     ]
     whole = pl.BlockSpec(memory_space=pltpu.HBM)
     scalars = pl.BlockSpec(memory_space=pltpu.SMEM)
     rows = jax.ShapeDtypeStruct((ROWS, WIDTH), F32)
+    blocks = [
+        pltpu.with_memory_space_constraint(array, pltpu.HBM)
+        for array in (queries[0], keys[0], values[0], out_grad[0], out_weight)
+    ]
+    head_offsets = pltpu.with_memory_space_constraint(head_offsets, pltpu.HBM)
     got = pl.pallas_call(
         kernel,
         out_shape=(
             jax.ShapeDtypeStruct((4, 3, 128, 128), F32),
             jax.ShapeDtypeStruct((4, 3, 64, 128), F32),
-            jax.ShapeDtypeStruct((16, 12, 128), F32),
+            jax.ShapeDtypeStruct((16, 6, 128), F32),
+            jax.ShapeDtypeStruct((16, 6, 128), F32),
         ),
         in_specs=[whole] * 5 + [scalars] * 2,
-        out_specs=(whole,) * 3,
+        out_specs=(whole,) * 4,
         scratch_shapes=scratch,
         compiler_params=pltpu.CompilerParams(
-            collective_id=0, has_side_effects=True, vmem_limit_bytes=60 * 1024 * 1024
+            collective_id=0, has_side_effects=True, vmem_limit_bytes=48 * 1024 * 1024
         ),
         cost_estimate=pl.CostEstimate(
             flops=4_000_000_000, bytes_accessed=4_000_000, transcendentals=1_000_000
         ),
         name="dilated_backward",
-    )(queries[0], keys[0], values[0], out_grad[0], out_weight, valid_tiles, head_offsets)
+    )(*blocks, valid_tiles, head_offsets)
     d_query, d_key, d_value, d_weight = pl.pallas_call(
         put_together,
         out_shape=(rows, rows, rows, jax.ShapeDtypeStruct((3, WIDTH), F32)),
-        in_specs=[whole] * 3 + [scalars],
+        in_specs=[pl.BlockSpec(memory_space=pltpu.VMEM)] * 4 + [scalars],
         out_specs=(whole,) * 4,
         scratch_shapes=[
-            block(4, 3, 128, 128), block(4, 3, 64, 128), block(16, 12, 128),
             block(ROWS, WIDTH), block(ROWS, WIDTH), block(ROWS, WIDTH), block(3, WIDTH),
-            pltpu.SemaphoreType.DMA((7,)), pltpu.SemaphoreType.DMA((4,)),
+            pltpu.SemaphoreType.DMA((4,)),
         ],
-        compiler_params=pltpu.CompilerParams(vmem_limit_bytes=60 * 1024 * 1024),
+        compiler_params=pltpu.CompilerParams(vmem_limit_bytes=16 * 1024 * 1024),
         cost_estimate=pl.CostEstimate(flops=1_000_000, bytes_accessed=2_500_000, transcendentals=0),
         name="put_together",
     )(*got, head_offsets)

time: 60.2 us -> 58.4 us (0.970)
  Pallas kernels: 58.7 us -> 56.8 us
    pallas_call x1, Pallas kernels: 3.1 us -> 1.93 us  [on_device(): pl.pallas_call(put_together, out_shape=(rows, rows, rows, jax.ShapeDtypeS...]
    pallas_call x1, Pallas kernels: 55.6 us -> 54.9 us  [on_device(): pl.pallas_call(kernel, out_shape=(jax.ShapeDtypeStruct((4, 3, 128, 128),...]
where the time goes in v4:
time: 58.4 us; the launch traced here: 58.3 us
  Pallas kernels  56.8 us (97%)
  between operations  1.45 us (2%)
    pallas_call x1, Pallas kernels, on_device(): pl.pallas_call(kernel, out_shape=(jax.ShapeDtypeStruct((4, 3, 128, 128),...  54.9 us
    pallas_call x1, Pallas kernels, on_device(): pl.pallas_call(put_together, out_shape=(rows, rows, rows, jax.ShapeDtypeS...  1.93 us

profile of v4, /device:TPU:1, one launch (start us, length us, event | category | flops | bytes accessed | tf_op | source)
XLA Modules:
  0.0 58.3 jit_solution(549281960218110612)
XLA Ops:
  1.3 54.9 %dilated_backward.1 = (f32[4,3,128,128]{3,2,1,0:T(8,128)S(1)}, f32[4,3,64,128]{3,2,1,0:T(8,128)S(1)}, f32[16,6,128]{2,1,0:T(8,128)S(1)}, f32[16,6,128]{2,1,0:T(8,128)S(1)}) custom-call(f32[128,768]{1,0:T(8,128)} %bitcast.7, f32[128,768]{1,0:T(8,128)} %bitcast.8, f32[128,768]{1,0:T(8,128)} %bitcast.9, f32[128,768]{1,0:T(8,128)} %bitcast.10, f32[3,768]{1,0:T(4,128)} %w_in.1, ...), custom_call_target="tpu_custom_call" | custom-call | flops 4000000000 | bytes 4000000 | tf_op jit(solution)/shard_map/dilated_backward/pallas_call | solution.py:692
  56.2 1.9 %put_together.1 = (f32[128,768]{1,0:T(8,128)}, f32[128,768]{1,0:T(8,128)}, f32[128,768]{1,0:T(8,128)}, f32[3,768]{1,0:T(4,128)}) custom-call(f32[4,3,128,128]{3,2,1,0:T(8,128)S(1)} %get-tuple-element.12.full_got, f32[4,3,64,128]{3,2,1,0:T(8,128)S(1)} %get-tuple-element.13.half_got, f32[16,6,128]{2,1,0:T(8,128)S(1)} %get-tuple-element.14.last_got, ...), custom_call_target="tpu_custom_call" | custom-call | flops 1000000 | bytes 2500000 | tf_op jit(solution)/shard_map/put_together/pallas_call | solution.py:711

commit v5 on v4

--- a/solution.py
+++ b/solution.py
@@ -19,7 +19,7 @@
 HEADS_HERE = 3
 KEYS = SEG + FAR
 G_CHUNKS = 4
-G_EARLY = 2
+G_EARLY = 1
 FAR_FIRST = (8, 7, 9, 6, 10, 5, 11, 4, 12, 3, 13, 2, 14, 1, 15)
 SENDS = 32
 
@@ -309,32 +309,8 @@
         g_forwarded.add([(part, part, seg_peer(1))])
     take_grad(seat_of(2))
 
-    w_full_moves.arrive()
-    w_mid_moves.arrive()
-    for tile, ref in ((0, w_full), (1, w_mid)):
-        columns = ref[...].reshape(WIDTH, 128)
-        if tile == 1:
-            columns = jnp.where(c == 1, flip(columns), columns)
-        high = columns.astype(BF16)
-        w_hi[:, lanes_of(tile)] = high
-        w_lo[:, lanes_of(tile)] = (columns - high.astype(F32)).astype(BF16)
-
     g_forwarded.arrive()
     take_grad(seat_of(3))
-    for tt in range(SEATS):
-        rows = slice(tt * 128, (tt + 1) * 128)
-        high, low = g_hi[rows, :], g_lo[rows, :]
-        out = dot(high, w_hi[...]) + dot(low, w_hi[...]) + dot(high, w_lo[...])
-        full, middle = out[:, 0:128], out[:, 128:256]
-        for h, block, upper in ((0, full, False), (1, full, True), (2, middle, False)):
-            both = pair(block, upper).astype(BF16)
-            do4[h, rows, 0:128] = both
-            do4[h, rows, 128:256] = both
-        turned = full.T
-        do_t[0, :, rows] = turned[0:64]
-        do_t[1, :, rows] = turned[64:128]
-        do_t[2, :, rows] = middle.T[0:64]
-
     def as_queries(h, rows, block, upper):
         both = pair(block * 0.125, upper).astype(BF16)
         q4[h, rows, 0:128] = both
@@ -468,6 +444,30 @@
                 wg_full[n, xx, yy] = block[yy * 48 + n * 24:yy * 48 + n * 24 + 24]
     wg_first = sum_first(wg_full, wg_full_1)
 
+    w_full_moves.arrive()
+    w_mid_moves.arrive()
+    for tile, ref in ((0, w_full), (1, w_mid)):
+        columns = ref[...].reshape(WIDTH, 128)
+        if tile == 1:
+            columns = jnp.where(c == 1, flip(columns), columns)
+        high = columns.astype(BF16)
+        w_hi[:, lanes_of(tile)] = high
+        w_lo[:, lanes_of(tile)] = (columns - high.astype(F32)).astype(BF16)
+
+    for tt in range(SEATS):
+        rows = slice(tt * 128, (tt + 1) * 128)
+        high, low = g_hi[rows, :], g_lo[rows, :]
+        out = dot(high, w_hi[...]) + dot(low, w_hi[...]) + dot(high, w_lo[...])
+        full, middle = out[:, 0:128], out[:, 128:256]
+        for h, block, upper in ((0, full, False), (1, full, True), (2, middle, False)):
+            both = pair(block, upper).astype(BF16)
+            do4[h, rows, 0:128] = both
+            do4[h, rows, 128:256] = both
+        turned = full.T
+        do_t[0, :, rows] = turned[0:64]
+        do_t[1, :, rows] = turned[64:128]
+        do_t[2, :, rows] = middle.T[0:64]
+
     full_out = Group(full_got.at[pl.ds(0, 3)])
     own_out = []
 
@@ -490,19 +490,6 @@
 
     values_0, values_1 = value_grad(0), value_grad(1)
     both_heads(values_0, values_1, 2)
-    score_grad(0)
-    score_grad(1)
-    keys_0, keys_1 = key_grad(0), key_grad(1)
-    both_heads(keys_0, keys_1, 1)
-    far_grad(0, keys_0, values_0)
-    far_grad(1, keys_1, values_1)
-    far_out = Group(
-        far_got,
-        [
-            (far_part.at[y_place(j), pl.ds(0, 2)], far_got.at[j - 1, pl.ds(0, 2)], y_peer(j))
-            for j in (2, 1, 3)
-        ],
-    )
 
     half_in_moves.arrive()
     for tt in range(SEATS):
@@ -526,13 +513,27 @@
             wg_mid[1, xx, yy] = packed[12:24]
 
     mid_first = sum_first(wg_mid, wg_mid_1)
+
+    score_grad(0)
+    score_grad(1)
+    keys_0, keys_1 = key_grad(0), key_grad(1)
+    both_heads(keys_0, keys_1, 1)
+    wg_first.arrive()
+    wg_second = sum_second(wg_full, wg_full_1, wg_full_sum, wg_full_2)
+    far_grad(0, keys_0, values_0)
+    far_grad(1, keys_1, values_1)
+    far_out = Group(
+        far_got,
+        [
+            (far_part.at[y_place(j), pl.ds(0, 2)], far_got.at[j - 1, pl.ds(0, 2)], y_peer(j))
+            for j in (2, 1, 3)
+        ],
+    )
     query_grad(0)
     query_grad(1)
     for tt in range(SEATS):
         full_send[tt, 0] = dq_t[0:2, :, tt * 128:(tt + 1) * 128].reshape(128, 128).T
     send_full(0)
-    wg_first.arrive()
-    wg_second = sum_second(wg_full, wg_full_1, wg_full_sum, wg_full_2)
     d_value = value_grad(2)
     score_grad(2)
     d_key = key_grad(2)
@@ -541,17 +542,24 @@
         (far_part.at[y_place(j), pl.ds(2, 1)], far_got.at[j - 1, pl.ds(2, 1)], y_peer(j))
         for j in (2, 1, 3)
     )
+    for tt in range(SEATS):
+        for n, part in ((1, d_key), (2, d_value)):
+            top, bottom = part[tt * 128:tt * 128 + 64], part[tt * 128 + 64:tt * 128 + 128]
+            half_send[tt, n] = jnp.where(low_lanes(top), top, bottom)
+    half_out = Group(
+        half_got.at[pl.ds(0, 3)],
+        [
+            (half_send.at[seat_of(d), pl.ds(1, 2)], half_got.at[t, pl.ds(1, 2)], seg_peer(d))
+            for d in (2, 3, 1)
+        ],
+    )
     mid_first.arrive()
     mid_second = sum_second(wg_mid, wg_mid_1, wg_mid_sum, wg_mid_2)
     query_grad(2)
     for tt in range(SEATS):
         block = dq_t[2, :, tt * 128:(tt + 1) * 128]
         block = jnp.concatenate([block, block], axis=0).T
-        low = low_lanes(block[0:64])
-        half_send[tt, 0] = jnp.where(low, block[0:64], block[64:128])
-        for n, part in ((1, d_key), (2, d_value)):
-            top, bottom = part[tt * 128:tt * 128 + 64], part[tt * 128 + 64:tt * 128 + 128]
-            half_send[tt, n] = jnp.where(low, top, bottom)
+        half_send[tt, 0] = jnp.where(low_lanes(block[0:64]), block[0:64], block[64:128])
 
     def to_owners(notes, got):
         return Group(
@@ -575,10 +583,7 @@
         rows = parts[mm // 4 % 2]
         last[mm, 3:6, :] = (rows if mm < 8 else flip(rows))[3 * (mm % 4):3 * (mm % 4) + 3]
     last_moves = to_owners(last, last_got)
-    half_out = Group(
-        half_got.at[pl.ds(0, 3)],
-        [(half_send.at[seat_of(d)], half_got.at[t], seg_peer(d)) for d in (2, 3, 1)],
-    )
+    half_out.add((half_send.at[seat_of(d), 0], half_got.at[t, 0], seg_peer(d)) for d in (2, 3, 1))
     keep_own(half_send.at[t], half_got.at[t])
     keep_own(last.at[m], last_got.at[m])
     keep_own(far_note.at[m], far_note_got.at[m])
@@ -676,7 +681,7 @@
         block(4, 3, 32, 128), block(3, 3, 32, 128),
         block(2, 4, 4, 24, 128), block(2, 3, 4, 24, 128), block(2, 4, 24, 128), block(2, 3, 24, 128),
         block(2, 4, 4, 12, 128), block(2, 3, 4, 12, 128), block(2, 4, 12, 128), block(2, 3, 12, 128),
-        block(16, 6, 128), block(16, 6, 128), block(3, 64, SEG),
+        block(16, 8, 128), block(16, 8, 128), block(3, 64, SEG),
         block(4, 3, 128, 128), block(4, 3, 64, 128),
         pltpu.SemaphoreType.DMA((SENDS,)), pltpu.SemaphoreType.DMA((SENDS,)),
         pltpu.SemaphoreType.DMA((11,)),
@@ -694,8 +699,8 @@
         out_shape=(
             jax.ShapeDtypeStruct((4, 3, 128, 128), F32),
             jax.ShapeDtypeStruct((4, 3, 64, 128), F32),
-            jax.ShapeDtypeStruct((16, 6, 128), F32),
-            jax.ShapeDtypeStruct((16, 6, 128), F32),
+            jax.ShapeDtypeStruct((16, 8, 128), F32),
+            jax.ShapeDtypeStruct((16, 8, 128), F32),
         ),
         in_specs=[whole] * 5 + [scalars] * 2,
         out_specs=(whole,) * 4,

time: 58.4 us -> 57.3 us (0.981)
  Pallas kernels: 56.8 us -> 55.7 us
    pallas_call x1, Pallas kernels: 54.9 us -> 53.8 us  [on_device(): pl.pallas_call(kernel, out_shape=(jax.ShapeDtypeStruct((4, 3, 128, 128),...]
where the time goes in v5:
time: 57.3 us; the launch traced here: 57.2 us
  Pallas kernels  55.7 us (97%)
  between operations  1.45 us (3%)
    pallas_call x1, Pallas kernels, on_device(): pl.pallas_call(kernel, out_shape=(jax.ShapeDtypeStruct((4, 3, 128, 128),...  53.8 us
    pallas_call x1, Pallas kernels, on_device(): pl.pallas_call(put_together, out_shape=(rows, rows, rows, jax.ShapeDtypeS...  1.93 us

profile of v5, /device:TPU:1, one launch (start us, length us, event | category | flops | bytes accessed | tf_op | source)
XLA Modules:
  0.0 57.2 jit_solution(11326313456808721779)
XLA Ops:
  1.3 53.8 %dilated_backward.1 = (f32[4,3,128,128]{3,2,1,0:T(8,128)S(1)}, f32[4,3,64,128]{3,2,1,0:T(8,128)S(1)}, f32[16,8,128]{2,1,0:T(8,128)S(1)}, f32[16,8,128]{2,1,0:T(8,128)S(1)}) custom-call(f32[128,768]{1,0:T(8,128)} %bitcast.7, f32[128,768]{1,0:T(8,128)} %bitcast.8, f32[128,768]{1,0:T(8,128)} %bitcast.9, f32[128,768]{1,0:T(8,128)} %bitcast.10, f32[3,768]{1,0:T(4,128)} %w_in.1, ...), custom_call_target="tpu_custom_call" | custom-call | flops 4000000000 | bytes 4000000 | tf_op jit(solution)/shard_map/dilated_backward/pallas_call | solution.py:697
  55.1 1.9 %put_together.1 = (f32[128,768]{1,0:T(8,128)}, f32[128,768]{1,0:T(8,128)}, f32[128,768]{1,0:T(8,128)}, f32[3,768]{1,0:T(4,128)}) custom-call(f32[4,3,128,128]{3,2,1,0:T(8,128)S(1)} %get-tuple-element.12.full_got, f32[4,3,64,128]{3,2,1,0:T(8,128)S(1)} %get-tuple-element.13.half_got, f32[16,8,128]{2,1,0:T(8,128)S(1)} %get-tuple-element.14.last_got, ...), custom_call_target="tpu_custom_call" | custom-call | flops 1000000 | bytes 2500000 | tf_op jit(solution)/shard_map/put_together/pallas_call | solution.py:716

commit v6 on v5

--- a/solution.py
+++ b/solution.py
@@ -84,13 +84,13 @@
 
 def kernel(
     q_in, k_in, v_in, g_in, w_in, valid_ref, offset_ref,
-    full_got, half_got, last_got, far_note_got,
+    full_got, half_got, last_got,
     q_own, k_own, v_own, w_own, half_in, half_seg, full_in, full_seg, g_seg,
     note, note_got, w_full, w_mid, w_hi, w_lo, far,
     q4, k4, v4, kt, vt, do4, do_t, attn_t, prob, prob_hi, prob_lo, ds_hi, ds_lo, g_hi, g_lo,
     far_part, far_got,
     wg_full, wg_full_1, wg_full_sum, wg_full_2, wg_mid, wg_mid_1, wg_mid_sum, wg_mid_2,
-    last, far_note, dq_t, full_send, half_send,
+    last, dq_t, full_send, half_send,
     send_sem, recv_sem, local_sem,
 ):
     x = lax.axis_index("dp")
@@ -575,8 +575,7 @@
     for h in range(HEADS_HERE):
         rows = far_part[y, h] + far_got[0, h] + far_got[1, h] + far_got[2, h]
         for mm in range(16):
-            far_note[mm, 2 * h:2 * h + 2, :] = rows[2 * mm:2 * mm + 2]
-    far_last = to_owners(far_note, far_note_got)
+            last[mm, 6 + 2 * h:8 + 2 * h, :] = rows[2 * mm:2 * mm + 2]
     mid_second.arrive()
     parts = sum_last(wg_mid_sum, wg_mid_2)
     for mm in range(16):
@@ -586,7 +585,6 @@
     half_out.add((half_send.at[seat_of(d), 0], half_got.at[t, 0], seg_peer(d)) for d in (2, 3, 1))
     keep_own(half_send.at[t], half_got.at[t])
     keep_own(last.at[m], last_got.at[m])
-    keep_own(far_note.at[m], far_note_got.at[m])
 
     for group in (
         w_full_moves, w_mid_moves, g_forwarded, full_in_moves, value_in_moves, half_in_moves,
@@ -596,13 +594,13 @@
     full_out.arrive()
     for copy in own_out:
         copy.wait()
-    for group in (far_last, last_moves, half_out):
+    for group in (last_moves, half_out):
         group.sent()
         group.arrive()
 
 
 def put_together(
-    full_got, half_got, last_got, far_got, offset_ref, dq_out, dk_out, dv_out, wg_out,
+    full_got, half_got, last_got, offset_ref, dq_out, dk_out, dv_out, wg_out,
     dq_own, dk_own, dv_own, wg_own, out_sem,
 ):
     stores = [
@@ -614,15 +612,15 @@
     row64 = lax.broadcasted_iota(jnp.int32, (64, 128), 0)
     low64 = lax.broadcasted_iota(jnp.int32, (64, 128), 1) < 64
     outs = (dq_own, dk_own, dv_own)
-    far_rows, wg_rows = [
-        [got[tt] + got[4 + tt] + got[8 + tt] + got[12 + tt] for tt in range(SEATS)]
-        for got in (far_got, last_got)
+    notes = [
+        last_got[tt] + last_got[4 + tt] + last_got[8 + tt] + last_got[12 + tt]
+        for tt in range(SEATS)
     ]
 
     def with_extra(n, r, tt, h, upper, block):
         if n == 0:
             return block
-        row = far_rows[tt][2 * h + r:2 * h + r + 1]
+        row = notes[tt][6 + 2 * h + r:7 + 2 * h + r]
         if (n == 2) != upper:
             row = flip(row)
         keep = (row64 == offset_ref[head_of(tt, h)]) & (low64 != upper)
@@ -649,9 +647,9 @@
 
     scale = 8192.0 ** -0.5
     for tt in range(SEATS):
-        wg_own[:, lanes_of(full_tile(tt))] = wg_rows[tt][0:3] * scale
+        wg_own[:, lanes_of(full_tile(tt))] = notes[tt][0:3] * scale
     for half in range(2):
-        even, odd = wg_rows[2 * half][3:6], wg_rows[2 * half + 1][3:6]
+        even, odd = notes[2 * half][3:6], notes[2 * half + 1][3:6]
         wg_own[:, lanes_of(3 * half + 1)] = jnp.where(low_lanes(even), even, flip(odd)) * scale
     stores[3].start()
     for copy in stores:
@@ -681,7 +679,7 @@
         block(4, 3, 32, 128), block(3, 3, 32, 128),
         block(2, 4, 4, 24, 128), block(2, 3, 4, 24, 128), block(2, 4, 24, 128), block(2, 3, 24, 128),
         block(2, 4, 4, 12, 128), block(2, 3, 4, 12, 128), block(2, 4, 12, 128), block(2, 3, 12, 128),
-        block(16, 8, 128), block(16, 8, 128), block(3, 64, SEG),
+        block(16, 12, 128), block(3, 64, SEG),
         block(4, 3, 128, 128), block(4, 3, 64, 128),
         pltpu.SemaphoreType.DMA((SENDS,)), pltpu.SemaphoreType.DMA((SENDS,)),
         pltpu.SemaphoreType.DMA((11,)),
@@ -699,11 +697,10 @@
         out_shape=(
             jax.ShapeDtypeStruct((4, 3, 128, 128), F32),
             jax.ShapeDtypeStruct((4, 3, 64, 128), F32),
-            jax.ShapeDtypeStruct((16, 8, 128), F32),
-            jax.ShapeDtypeStruct((16, 8, 128), F32),
+            jax.ShapeDtypeStruct((16, 12, 128), F32),
         ),
         in_specs=[whole] * 5 + [scalars] * 2,
-        out_specs=(whole,) * 4,
+        out_specs=(whole,) * 3,
         scratch_shapes=scratch,
         compiler_params=pltpu.CompilerParams(
             collective_id=0, has_side_effects=True, vmem_limit_bytes=48 * 1024 * 1024
@@ -716,7 +713,7 @@
     d_query, d_key, d_value, d_weight = pl.pallas_call(
         put_together,
         out_shape=(rows, rows, rows, jax.ShapeDtypeStruct((3, WIDTH), F32)),
-        in_specs=[pl.BlockSpec(memory_space=pltpu.VMEM)] * 4 + [scalars],
+        in_specs=[pl.BlockSpec(memory_space=pltpu.VMEM)] * 3 + [scalars],
         out_specs=(whole,) * 4,
         scratch_shapes=[
             block(ROWS, WIDTH), block(ROWS, WIDTH), block(ROWS, WIDTH), block(3, WIDTH),

time: 57.3 us -> 56.6 us (0.988)
  Pallas kernels: 55.7 us -> 55 us
    pallas_call x1, Pallas kernels: 53.8 us -> 53.1 us  [on_device(): pl.pallas_call(kernel, out_shape=(jax.ShapeDtypeStruct((4, 3, 128, 128),...]
where the time goes in v6:
time: 56.6 us; the launch traced here: 56.4 us
  Pallas kernels  55 us (97%)
  between operations  1.45 us (3%)
    pallas_call x1, Pallas kernels, on_device(): pl.pallas_call(kernel, out_shape=(jax.ShapeDtypeStruct((4, 3, 128, 128),...  53.1 us
    pallas_call x1, Pallas kernels, on_device(): pl.pallas_call(put_together, out_shape=(rows, rows, rows, jax.ShapeDtypeS...  1.93 us

profile of v6, /device:TPU:1, one launch (start us, length us, event | category | flops | bytes accessed | tf_op | source)
XLA Modules:
  0.0 56.4 jit_solution(17151893454667814502)
XLA Ops:
  1.3 53.1 %dilated_backward.1 = (f32[4,3,128,128]{3,2,1,0:T(8,128)S(1)}, f32[4,3,64,128]{3,2,1,0:T(8,128)S(1)}, f32[16,12,128]{2,1,0:T(8,128)S(1)}) custom-call(f32[128,768]{1,0:T(8,128)} %bitcast.7, f32[128,768]{1,0:T(8,128)} %bitcast.8, f32[128,768]{1,0:T(8,128)} %bitcast.9, f32[128,768]{1,0:T(8,128)} %bitcast.10, f32[3,768]{1,0:T(4,128)} %w_in.1, ...), custom_call_target="tpu_custom_call" | custom-call | flops 4000000000 | bytes 4000000 | tf_op jit(solution)/shard_map/dilated_backward/pallas_call | solution.py:695
  54.3 1.9 %put_together.1 = (f32[128,768]{1,0:T(8,128)}, f32[128,768]{1,0:T(8,128)}, f32[128,768]{1,0:T(8,128)}, f32[3,768]{1,0:T(4,128)}) custom-call(f32[4,3,128,128]{3,2,1,0:T(8,128)S(1)} %get-tuple-element.11.full_got, f32[4,3,64,128]{3,2,1,0:T(8,128)S(1)} %get-tuple-element.12.half_got, f32[16,12,128]{2,1,0:T(8,128)S(1)} %get-tuple-element.13.last_got, s32[12]{0:T(128)} %offset_ref.3), custom_call_target="tpu_custom_call" | custom-call | flops 1000000 | bytes 2500000 | tf_op jit(solution)/shard_map/put_together/pallas_call | solution.py:713

commit v7 on v6

--- a/solution.py
+++ b/solution.py
@@ -18,8 +18,8 @@
 WIDTH = 768
 HEADS_HERE = 3
 KEYS = SEG + FAR
-G_CHUNKS = 4
-G_EARLY = 1
+G_CHUNKS = 2
+G_EARLY = 0
 FAR_FIRST = (8, 7, 9, 6, 10, 5, 11, 4, 12, 3, 13, 2, 14, 1, 15)
 SENDS = 32
 

time: 56.6 us -> 56.9 us (level)
  no operation moved by 1% of the time
where the time goes in v7:
time: 56.9 us; the launch traced here: 56.8 us
  Pallas kernels  55.3 us (97%)
  between operations  1.45 us (3%)
    pallas_call x1, Pallas kernels, on_device(): pl.pallas_call(kernel, out_shape=(jax.ShapeDtypeStruct((4, 3, 128, 128),...  53.4 us
    pallas_call x1, Pallas kernels, on_device(): pl.pallas_call(put_together, out_shape=(rows, rows, rows, jax.ShapeDtypeS...  1.93 us

profile of v7, /device:TPU:1, one launch (start us, length us, event | category | flops | bytes accessed | tf_op | source)
XLA Modules:
  0.0 56.8 jit_solution(12931295917744077333)
XLA Ops:
  1.3 53.4 %dilated_backward.1 = (f32[4,3,128,128]{3,2,1,0:T(8,128)S(1)}, f32[4,3,64,128]{3,2,1,0:T(8,128)S(1)}, f32[16,12,128]{2,1,0:T(8,128)S(1)}) custom-call(f32[128,768]{1,0:T(8,128)} %bitcast.7, f32[128,768]{1,0:T(8,128)} %bitcast.8, f32[128,768]{1,0:T(8,128)} %bitcast.9, f32[128,768]{1,0:T(8,128)} %bitcast.10, f32[3,768]{1,0:T(4,128)} %w_in.1, ...), custom_call_target="tpu_custom_call" | custom-call | flops 4000000000 | bytes 4000000 | tf_op jit(solution)/shard_map/dilated_backward/pallas_call | solution.py:695
  54.7 1.9 %put_together.1 = (f32[128,768]{1,0:T(8,128)}, f32[128,768]{1,0:T(8,128)}, f32[128,768]{1,0:T(8,128)}, f32[3,768]{1,0:T(4,128)}) custom-call(f32[4,3,128,128]{3,2,1,0:T(8,128)S(1)} %get-tuple-element.11.full_got, f32[4,3,64,128]{3,2,1,0:T(8,128)S(1)} %get-tuple-element.12.half_got, f32[16,12,128]{2,1,0:T(8,128)S(1)} %get-tuple-element.13.last_got, s32[12]{0:T(128)} %offset_ref.3), custom_call_target="tpu_custom_call" | custom-call | flops 1000000 | bytes 2500000 | tf_op jit(solution)/shard_map/put_together/pallas_call | solution.py:713
